TPU v7x, 256 devices: a whole 4x4x8 slice. The times are simulated.
256 devices in a mesh: rep: 64 (over x, y_hi, z), fsdp: 4 (over y_lo, core).
Axes of the slice: x: 4, y: 4 (y_hi: 2, y_lo: 2; y = y_hi * 2 + y_lo), z: 8, core: 2. Of those that a mesh axis runs over, the one named last changes fastest.
Arguments:
- hidden: bfloat16 [64, 1024, 4608], P('rep', 'fsdp'), may hold values from -6 to 6
- upstream: bfloat16 [64, 1024, 1024], P('rep', 'fsdp'), may hold values from -6 to 6
- weights: bfloat16 [64, 4608, 1024], P('rep', 'fsdp'), may hold values from -16 to 16
- moment_one: bfloat16 [64, 4608, 1024], P('rep', 'fsdp'), may hold values from -0.59765625 to 0.59765625
- moment_two: bfloat16 [64, 4608, 1024], P('rep', 'fsdp'), may hold values from 0.0029907227 to 0.099609375
- global_params: float32 [4, 1152, 1024], P('fsdp', 'rep'), may hold values from -6 to 6
- outer_momentum: float32 [4, 1152, 1024], P('fsdp', 'rep'), may hold values from -2 to 2
Outputs:
- values: bfloat16 [64, 1024, 1024], P('rep', 'fsdp')
- merged: bfloat16 [64, 4608, 1024], P('rep', 'fsdp')
- new_global: float32 [4, 1152, 1024], P('fsdp', 'rep')
- new_momentum: float32 [4, 1152, 1024], P('fsdp', 'rep')
All inputs are finite; a program needn't handle non-finite values.
Results may differ from a plain program's by a relative error of at most 0.007.
Values may be sent and summed in bfloat16 or wider, within the bound.
No kernel may reach another device: no remote copies, remote signals or barrier semaphores. Data moves between devices by JAX's collectives and lax.ppermute only.
A program may use at most 128 MiB of HBM per device.

v0:
```python
import jax
import jax.numpy as jnp
from jax import lax
from jax.sharding import PartitionSpec as P

beta_one = 0.9
beta_two = 0.95
bias_one = 1.0 - 0.9**8
bias_two = 1.0 - 0.95**8
inner_rate = 0.25
decay_rate = 0.1
epsilon = 1e-08
outer_rate = 0.7
outer_mu = 0.9
mixing = 0.5


def on_device(hidden, upstream, weights, moment_one, moment_two, global_params, outer_momentum):
    factor = float(hidden.shape[2]) ** (-0.5)
    tokens = hidden[0]
    grads_in = upstream[0]
    local_rows = weights[0]
    selected = tokens
    projected = jnp.dot(
        selected,
        lax.all_gather(weights, "fsdp", axis=1, tiled=True)[0],
        preferred_element_type=jnp.float32,
    )
    values = (projected * factor).astype(jnp.bfloat16)
    selected = tokens
    gradient = lax.psum_scatter(
        (
            lax.dot_general(
                selected, grads_in, (((0,), (0,)), ((), ())), preferred_element_type=jnp.float32
            )
            * factor
        ).astype(jnp.bfloat16),
        "fsdp",
        scatter_dimension=0,
        tiled=True,
    ).astype(jnp.float32)
    moment_new = beta_one * moment_one[0].astype(jnp.float32) + (1.0 - beta_one) * gradient
    second_new = (
        beta_two * moment_two[0].astype(jnp.float32) + (1.0 - beta_two) * gradient * gradient
    )
    stepped = moment_new / bias_one / (jnp.sqrt(second_new / bias_two) + epsilon)
    current = local_rows.astype(jnp.float32)
    updated = current - inner_rate * (stepped + decay_rate * current)
    summed = lax.psum(weights.astype(jnp.float32), "rep")
    owned_rows = global_params.shape[1]
    owned = lax.dynamic_slice_in_dim(summed, lax.axis_index("rep") * owned_rows, owned_rows, 1)
    pseudo = global_params - owned / lax.axis_size("rep")
    momentum = outer_mu * outer_momentum + pseudo
    renewed = global_params - outer_rate * (pseudo + outer_mu * momentum)
    spread = lax.all_gather(renewed.astype(jnp.bfloat16), "rep", axis=1, tiled=True).astype(
        renewed.dtype
    )[0]
    merged = (mixing * updated + (1.0 - mixing) * spread).astype(jnp.bfloat16)
    return (values[None], merged[None], renewed, momentum)


def solution(mesh):
    return jax.shard_map(
        on_device,
        mesh=mesh,
        in_specs=(
            P("rep", "fsdp", None),
            P("rep", "fsdp", None),
            P("rep", "fsdp", None),
            P("rep", "fsdp", None),
            P("rep", "fsdp", None),
            P("fsdp", "rep", None),
            P("fsdp", "rep", None),
        ),
        out_specs=(
            P("rep", "fsdp", None),
            P("rep", "fsdp", None),
            P("fsdp", "rep", None),
            P("fsdp", "rep", None),
        ),
        check_vma=False,
    )
```

profile of v0, /device:TPU:32, one launch (start us, length us, event | category | flops | bytes accessed | tf_op | source)
XLA Modules:
  0.0 651.6 jit_solution(4639280205007164446)
XLA Ops:
  7.2 0.0 copy-start
  7.2 0.0 copy-start.1
  7.2 0.0 copy-start.2
  7.2 0.0 copy-start.3
  7.2 0.0 all-gather.3.cloned.1.call-start
  7.3 0.7 all-gather.3.cloned.1.call-update
  7.9 0.0 all-gather.5.cloned.1.call-start
  8.0 406.9 %all-reduce.1 = f32[1,1152,1024]{2,1,0:T(8,128)} all-reduce(bf16[1,1152,1024]{2,1,0:T(8,128)(2,1)} %param.9), channel_id=1, replica_groups=mesh['rep'=64,'fsdp'=4] {'rep'}, use_global_device_ids=true, to_apply=%region_1.0 | all-reduce | flops 1179648 | bytes 7077888 | tf_op jit(solution)/shard_map/psum | solution.py:49
  414.9 0.0 copy-done.1
  414.9 0.0 copy-done.2
  414.9 1.0 fusion.33
  415.9 0.7 copy.19
  416.6 0.0 all-gather.5.cloned.1.call-update
  416.6 0.0 reduce-scatter.2.cloned.1.call-start
  416.6 0.0 copy-done
  416.6 0.0 copy-done.3
  416.7 5.1 multiply_convert_fusion
  421.8 0.0 reduce-scatter.2.cloned.1.call-update
  421.8 0.7 copy.21
  422.5 0.7 copy.22
  423.2 7.1 %fusion.26 = bf16[1,256,1024]{2,1,0:T(8,128)(2,1)} fusion(bf16[1,4608,1024]{2,1,0:T(8,128)(2,1)} %all-gather.3.cloned.1.call-done, bf16[1,256,4608]{2,1,0:T(8,128)(2,1)S(1)} %copy-done), kind=kOutput, calls=%fused_computation.23 | convolution fusion | flops 2416443392 | bytes 12320768 | tf_op jit(solution)/shard_map/dot_general | solution.py:24
  430.3 116.0 %all-gather.5.cloned.1.call-done = bf16[1,1152,1024]{2,0,1:T(2,128)(2,1)} async-done(((bf16[1,18,1024]{2,0,1:T(2,128)(2,1)}), bf16[1,1152,1024]{2,0,1:T(2,128)(2,1)}) %all-gather.5.cloned.1.call-update) | async-done | bytes 2359312 | tf_op jit(solution)/shard_map/all_gather | solution.py:55
  546.3 89.7 %reduce-scatter.2.cloned.1.call-done = bf16[1152,1024]{1,0:T(8,128)(2,1)} async-done(((bf16[4608,1024]{1,0:T(8,128)(2,1)}), bf16[1152,1024]{1,0:T(8,128)(2,1)}) %reduce-scatter.2.cloned.1.call-update) | async-done | bytes 2359312 | tf_op jit(solution)/shard_map/reduce_scatter | solution.py:31
  636.0 9.0 %fusion.15 = bf16[1,1152,1024]{2,1,0:T(8,128)(2,1)} fusion(bf16[1,1152,1024]{2,0,1:T(2,128)(2,1)} %all-gather.5.cloned.1.call-done, bf16[1,1152,1024]{2,1,0:T(8,128)(2,1)} %param.11, bf16[1152,1024]{1,0:T(8,128)(2,1)} %reduce-scatter.2.cloned.1.call-done, bf16[1,1152,1024]{2,1,0:T(8,128)(2,1)} %param.10, bf16[1,1152,1024]{2,1,0:T(8,128)(2,1)} %param.9), kind=kLoop, calls=%fused_computation.20 | loop fusion | flops 27131904 | bytes 14155776 | tf_op jit(solution)/shard_map/broadcast_in_dim | solution.py:59
  (1 shorter events, 0.0 us)
Async XLA Ops:
  7.2 409.5 %copy-start = (bf16[1,256,4608]{2,1,0:T(8,128)(2,1)S(1)}, bf16[1,256,4608]{2,1,0:T(8,128)(2,1)}, u32[]{:S(2)}) copy-start(bf16[1,256,4608]{2,1,0:T(8,128)(2,1)} %param.7) | copy-start | bytes 7077892
  7.2 407.7 %copy-start.1 = (f32[1,18,1024]{2,0,1:T(1,128)S(1)}, f32[1,18,1024]{2,0,1:T(1,128)}, u32[]{:S(2)}) copy-start(f32[1,18,1024]{2,0,1:T(1,128)} %param.12) | copy-start | bytes 221188
  7.2 407.7 %copy-start.2 = (f32[1,18,1024]{2,0,1:T(1,128)S(1)}, f32[1,18,1024]{2,0,1:T(1,128)}, u32[]{:S(2)}) copy-start(f32[1,18,1024]{2,0,1:T(1,128)} %param.13) | copy-start | bytes 221188
  7.2 409.5 %copy-start.3 = (bf16[1,256,1024]{2,1,0:T(8,128)(2,1)S(1)}, bf16[1,256,1024]{2,1,0:T(8,128)(2,1)}, u32[]{:S(2)}) copy-start(bf16[1,256,1024]{2,1,0:T(8,128)(2,1)} %param.8) | copy-start | bytes 1572868
  7.2 416.0 %all-gather.3.cloned.1.call-start = ((), (), s32[]{:S(2)}) async-start(), calls=%async_computation.1 | async-start | bytes 11796480 | tf_op jit(solution)/shard_map/all_gather | solution.py:26
  7.9 538.4 %all-gather.5.cloned.1.call-start = ((), (), s32[]{:S(2)}) async-start(), calls=%async_computation.3 | async-start | bytes 4792320 | tf_op jit(solution)/shard_map/all_gather | solution.py:55
  416.6 219.4 %reduce-scatter.2.cloned.1.call-start = ((), (), s32[]{:S(2)}) async-start(), calls=%async_computation.2 | async-start | bytes 11796480 | tf_op jit(solution)/shard_map/reduce_scatter | solution.py:31
Sparse Core Ops, SparseCore 0:
  9.8 93.8 all-gather.2
  416.7 129.5 all-gather.4
  549.0 87.0 reduce-scatter.1
where the time goes:
time: 653 us; the launch traced here: 652 us
  blocking collectives  407 us (62%)
  waiting for transfers between devices  206 us (32%)
  between operations  13.8 us (2%)
  matrix products  12.2 us (2%)
  other arithmetic  9.97 us (2%)
    psum x1, blocking collectives, on_device(): summed = lax.psum(weights.astype(jnp.float32), 'rep')  407 us
    all_gather x1, waiting for transfers between devices, on_device(): lax.all_gather(renewed.astype(jnp.bfloat16), 'rep', axis=1, tiled=True)  116 us
    reduce_scatter x1, waiting for transfers between devices, on_device(): lax.psum_scatter((lax.dot_general(selected, grads_in, (((0,), (0,)), ((),...  89.7 us
  transfers between devices with their start and end apart: 3, of which 2 were waited for; matrix products, arithmetic and copies ran while one was open for 2% of the time, Pallas kernels for 0%

commit v1 on v0

v1 whole, which is shorter than its diff:
```python
import jax
import jax.numpy as jnp
from jax import lax
from jax.sharding import PartitionSpec as P

beta_one = 0.9
beta_two = 0.95
bias_one = 1.0 - 0.9**8
bias_two = 1.0 - 0.95**8
inner_rate = 0.25
decay_rate = 0.1
epsilon = 1e-08
outer_rate = 0.7
outer_mu = 0.9
mixing = 0.5

NX, NYH, NZ = 4, 2, 8
NYL, NC = 2, 2
BOTH = ("rep", "fsdp")
X_GROUPS = [[(x * NYH + h) * NZ + z for x in range(NX)] for h in range(NYH) for z in range(NZ)]
Z_GROUPS = [[(x * NYH + h) * NZ + z for z in range(NZ)] for x in range(NX) for h in range(NYH)]


def pairs(move):
    found = []
    for x in range(NX):
        for h in range(NYH):
            for z in range(NZ):
                for y in range(NYL):
                    for c in range(NC):
                        h2, y2, c2 = move(h, y, c)
                        found.append(
                            (
                                ((x * NYH + h) * NZ + z) * 4 + y * 2 + c,
                                ((x * NYH + h2) * NZ + z) * 4 + y2 * 2 + c2,
                            )
                        )
    return found


TO_OTHER_CORE = pairs(lambda h, y, c: (h, y, 1 - c))
TO_OTHER_CHIP = pairs(lambda h, y, c: (h, 1 - y, c))
TO_OTHER_HALF = pairs(lambda h, y, c: (1 - h, y, c))


def over_x(array):
    return lax.all_to_all(array, "rep", 0, 0, axis_index_groups=X_GROUPS)


def over_z(array):
    return lax.all_to_all(array, "rep", 0, 0, axis_index_groups=Z_GROUPS)


def swap(array, to):
    return lax.ppermute(array, BOTH, to)


def dot(a, b, contract=((1,), (0,))):
    return lax.dot_general(a, b, (contract, ((), ())), preferred_element_type=jnp.float32)


def on_device(hidden, upstream, weights, moment_one, moment_two, global_params, outer_momentum):
    bf16, f32 = jnp.bfloat16, jnp.float32
    tokens, width = hidden.shape[1:]
    rows, cols = weights.shape[1:]
    factor = float(width) ** (-0.5)
    own_rows = global_params.shape[1]
    block = rows // NX
    lane = cols // NZ
    half = block // NYH
    chip = width // NYL
    rep, fsdp = lax.axis_index("rep"), lax.axis_index("fsdp")
    core, pair = fsdp % NC, fsdp // NC
    side = (rep // NZ) % NYH

    w = weights[0]
    h = hidden[0]
    u = upstream[0]

    parts_x = over_x(w.reshape(NX, block, cols))

    h_sent = lax.dynamic_slice_in_dim(h, (1 - pair) * chip, chip, 1)
    h_kept = lax.dynamic_slice_in_dim(h, pair * chip, chip, 1)
    h_got = swap(h_sent, TO_OTHER_CHIP)
    u_got = swap(u, TO_OTHER_CHIP)
    w_other = swap(w, TO_OTHER_CORE)

    state = jnp.stack([global_params[0], outer_momentum[0]]).reshape(2, own_rows, NZ, lane)
    state = over_z(state.transpose(2, 0, 1, 3))
    state = state.transpose(1, 0, 2, 3).reshape(2, half, lane)
    state_far = swap(state, TO_OTHER_HALF)
    first = jnp.where(side == 0, state, state_far)
    second = jnp.where(side == 0, state_far, state)
    state = jnp.concatenate([first, second], axis=1)

    sum_x = jnp.sum(parts_x.astype(f32), axis=0).astype(bf16)
    parts_z = over_z(sum_x.reshape(block, NZ, lane).transpose(1, 0, 2))
    sum_z = jnp.sum(parts_z.astype(f32), axis=0)
    summed = sum_z + swap(sum_z.astype(bf16), TO_OTHER_HALF).astype(f32)
    pseudo = state[0] - summed / lax.axis_size("rep")
    momentum = outer_mu * state[1] + pseudo
    renewed = (state[0] - outer_rate * (pseudo + outer_mu * momentum)).astype(bf16)

    owned = lax.dynamic_slice_in_dim(summed, side * half, half, 0).astype(bf16)
    owned = jnp.pad(owned.reshape(NZ, own_rows, lane), ((0, 0), (0, 32 - own_rows), (0, 0)))
    spread_z = over_z(
        jnp.concatenate([jnp.broadcast_to(renewed, (NZ, block, lane)), owned], axis=1)
    )
    spread = over_x(jnp.broadcast_to(spread_z[:, :block], (NX, NZ, block, lane)))
    spread = spread.transpose(0, 2, 1, 3).reshape(rows, cols)

    owned = spread_z[:, block : block + own_rows].transpose(1, 0, 2).reshape(own_rows, cols)
    pseudo = global_params[0] - owned.astype(f32) / lax.axis_size("rep")
    new_momentum = outer_mu * outer_momentum[0] + pseudo
    new_global = global_params[0] - outer_rate * (pseudo + outer_mu * new_momentum)

    def project(part):
        mine = lax.dynamic_slice_in_dim(part, core * rows, rows, 1)
        theirs = lax.dynamic_slice_in_dim(part, (1 - core) * rows, rows, 1)
        return (dot(mine, w) + dot(theirs, w_other)) * factor

    far = swap(project(h_got).astype(bf16), TO_OTHER_CHIP)
    values = (project(h_kept) + far.astype(f32)).astype(bf16)

    def mine_of(part):
        return lax.dynamic_slice_in_dim(part, core * rows, rows, 1)

    def theirs_of(part):
        return lax.dynamic_slice_in_dim(part, (1 - core) * rows, rows, 1)

    near_other = swap(theirs_of(h_kept), TO_OTHER_CORE)
    u_other = swap(u, TO_OTHER_CORE)
    far_other = swap(theirs_of(h_got), TO_OTHER_CORE)
    u_far_other = swap(u_got, TO_OTHER_CORE)
    t = ((0,), (0,))
    gradient = dot(mine_of(h_kept), u, t) + dot(near_other, u_other, t)
    gradient = gradient + dot(mine_of(h_got), u_got, t) + dot(far_other, u_far_other, t)
    gradient = gradient * factor

    moment_new = beta_one * moment_one[0].astype(f32) + (1.0 - beta_one) * gradient
    second_new = beta_two * moment_two[0].astype(f32) + (1.0 - beta_two) * gradient * gradient
    stepped = moment_new / bias_one / (jnp.sqrt(second_new / bias_two) + epsilon)
    current = w.astype(f32)
    updated = current - inner_rate * (stepped + decay_rate * current)
    merged = (mixing * updated + (1.0 - mixing) * spread.astype(f32)).astype(bf16)
    return (values[None], merged[None], new_global[None], new_momentum[None])


def solution(mesh):
    return jax.shard_map(
        on_device,
        mesh=mesh,
        in_specs=(
            P("rep", "fsdp", None),
            P("rep", "fsdp", None),
            P("rep", "fsdp", None),
            P("rep", "fsdp", None),
            P("rep", "fsdp", None),
            P("fsdp", "rep", None),
            P("fsdp", "rep", None),
        ),
        out_specs=(
            P("rep", "fsdp", None),
            P("rep", "fsdp", None),
            P("fsdp", "rep", None),
            P("fsdp", "rep", None),
        ),
        check_vma=False,
    )
```

time: 653 us -> 176 us (0.27)
  blocking collectives: 407 us -> 0 us
  waiting for transfers between devices: 206 us -> 82.8 us
  starting transfers between devices: 0.12 us -> 37.6 us
  matrix products: 12.2 us -> 33.2 us
  between operations: 13.8 us -> 0.91 us
  local copies, waits for them, and re-layouts: 2.13 us -> 11.3 us
    psum x1 -> x0, blocking collectives: 407 us -> none  [on_device(): summed = lax.psum(weights.astype(jnp.float32), 'rep')]
    all_gather x2 -> x0, waiting for transfers between devices: 116 us -> none  [the longest x1 116 us: on_device(): lax.all_gather(renewed.astype(jnp.bfloat16), 'rep', axis=1, tiled=True)]
    reduce_scatter x1 -> x0, waiting for transfers between devices: 89.7 us -> none  [on_device(): lax.psum_scatter((lax.dot_general(selected, grads_in, (((0,), (0,)), ((),...]
    all_to_all x0 -> x5, waiting for transfers between devices: none -> 55.3 us  [the longest x2 43.8 us: over_x(): return lax.all_to_all(array, 'rep', 0, 0, axis_index_groups=X_GROUPS)]
    all_to_all x0 -> x5, starting transfers between devices: none -> 29.8 us  [the longest x3 20.7 us: over_z(): return lax.all_to_all(array, 'rep', 0, 0, axis_index_groups=Z_GROUPS)]
    ppermute x0 -> x10, waiting for transfers between devices: none -> 27.5 us  [swap(): return lax.ppermute(array, BOTH, to)]
    dot_general x2 -> x8, matrix products: 12.2 us -> 33.2 us  [dot(): lax.dot_general(a, b, (contract, ((), ())), preferred_element_type=jnp.fl...]
    broadcast_in_dim x1 -> x0, other arithmetic: 9.01 us -> none  [on_device(): return (values[None], merged[None], renewed, momentum)]
  transfers between devices with their start and end apart: 3 -> 15, of which waited for: 2 -> 6; matrix products, arithmetic and copies ran while one was open for 2% -> 24% of each run, Pallas kernels for 0% -> 0%
where the time goes in v1:
time: 176 us; the launch traced here: 173 us
  waiting for transfers between devices  82.8 us (47%)
  starting transfers between devices  37.6 us (21%)
  matrix products  33.2 us (19%)
  local copies, waits for them, and re-layouts  11.3 us (6%)
  other arithmetic  7.37 us (4%)
    all_to_all x2, waiting for transfers between devices, over_x(): return lax.all_to_all(array, 'rep', 0, 0, axis_index_groups=X_GROUPS)  43.8 us
    dot_general x8, matrix products, dot(): lax.dot_general(a, b, (contract, ((), ())), preferred_element_type=jnp.fl...  33.2 us
    ppermute x10, waiting for transfers between devices, swap(): return lax.ppermute(array, BOTH, to)  27.5 us
    all_to_all x3, starting transfers between devices, over_z(): return lax.all_to_all(array, 'rep', 0, 0, axis_index_groups=Z_GROUPS)  20.7 us
    all_to_all x3, waiting for transfers between devices, over_z(): return lax.all_to_all(array, 'rep', 0, 0, axis_index_groups=Z_GROUPS)  11.5 us
    all_to_all x2, starting transfers between devices, over_x(): return lax.all_to_all(array, 'rep', 0, 0, axis_index_groups=X_GROUPS)  9.14 us
    ppermute x10, starting transfers between devices, swap(): return lax.ppermute(array, BOTH, to)  7.77 us
  transfers between devices with their start and end apart: 15, of which 6 were waited for; matrix products, arithmetic and copies ran while one was open for 24% of the time, Pallas kernels for 0%

profile of v1, /device:TPU:32, one launch (start us, length us, event | category | flops | bytes accessed | tf_op | source)
XLA Modules:
  0.0 173.2 jit_solution(16145071280931857115)
XLA Ops:
  0.7 4.7 %all-to-all-start.1 = ((bf16[4,288,1024]{2,1,0:T(8,128)(2,1)}), bf16[4,288,1024]{2,1,0:T(8,128)(2,1)}, u32[]{:S(2)}, u32[]{:S(2)}) async-start(bf16[4,288,1024]{2,1,0:T(8,128)(2,1)} %bitcast.83), calls=%async_computation.1 | async-start | bytes 4718592 | tf_op jit(solution)/shard_map/all_to_all | solution.py:47
  6.1 28.7 %all-to-all-done.1 = bf16[4,288,1024]{2,1,0:T(8,128)(2,1)} async-done(((bf16[4,288,1024]{2,1,0:T(8,128)(2,1)}), bf16[4,288,1024]{2,1,0:T(8,128)(2,1)}, u32[]{:S(2)}, u32[]{:S(2)}) %all-to-all-start.1) | async-done | bytes 2359328 | tf_op jit(solution)/shard_map/all_to_all | solution.py:47
  34.8 8.6 %all-to-all-start = ((f32[8,2,18,128]{3,1,2,0:T(2,128)}), f32[8,2,18,128]{3,1,2,0:T(2,128)S(1)}, u32[]{:S(2)}, u32[]{:S(2)}) async-start(f32[8,2,18,128]{3,1,2,0:T(2,128)} %bitcast_bitcast_fusion), calls=%async_computation | async-start | bytes 294912 | tf_op jit(solution)/shard_map/all_to_all | solution.py:51
  45.2 2.2 %reduce_sum.21 = bf16[288,1024]{1,0:T(8,128)(2,1)S(1)} reduce(bf16[4,288,1024]{2,1,0:T(8,128)(2,1)} %all-to-all-done.1, bf16[]{:T(256)} %constant.124.clone.1), dimensions={0}, to_apply=%region_0.1 | reduce | flops 884736 | bytes 2949122 | tf_op jit(solution)/shard_map/reduce_sum | solution.py:96
  48.3 2.8 %all-to-all-done = f32[8,2,18,128]{3,1,2,0:T(2,128)S(1)} async-done(((f32[8,2,18,128]{3,1,2,0:T(2,128)}), f32[8,2,18,128]{3,1,2,0:T(2,128)S(1)}, u32[]{:S(2)}, u32[]{:S(2)}) %all-to-all-start) | async-done | bytes 147488 | tf_op jit(solution)/shard_map/all_to_all | solution.py:51
  51.2 4.9 %all-to-all-start.2 = ((bf16[8,288,128]{2,1,0:T(8,128)(2,1)}), bf16[8,288,128]{2,1,0:T(8,128)(2,1)S(1)}, u32[]{:S(2)}, u32[]{:S(2)}) async-start(bf16[8,288,128]{2,1,0:T(8,128)(2,1)} %copy.19), calls=%async_computation.2 | async-start | bytes 1179648 | tf_op jit(solution)/shard_map/all_to_all | solution.py:51
  58.7 4.2 %fusion.19 = f32[1152,1024]{1,0:T(8,128)} fusion(bf16[1,256,4608]{2,1,0:T(8,128)(2,1)S(1)} %copy-done, s32[]{:T(128)S(6)} %dynamic_slice.33, bf16[1,256,1024]{2,1,0:T(8,128)(2,1)} %param.8), kind=kOutput, calls=%fused_computation.31 | convolution fusion | flops 603979776 | bytes 5832708 | tf_op jit(solution)/shard_map/dot_general | solution.py:59
  63.0 2.9 %collective-permute-start.8 = (f32[2,144,128]{2,0,1:T(2,128)S(1)}, f32[2,144,128]{2,0,1:T(2,128)S(1)}, u32[]{:S(2)}, u32[]{:S(2)}) collective-permute-start(f32[2,144,128]{2,0,1:T(2,128)S(1)} %bitcast.88), channel_id=1, source_target_pairs={{0,32},{1,33},{2,34},{3,35},{4,36},{5,37},{6,38},{7,39},{8,40},{9,... | collective-permute-start | bytes 442376 | tf_op jit(solution)/shard_map/ppermute | solution.py:55
  66.9 22.3 %collective-permute-done.8 = f32[2,144,128]{2,0,1:T(2,128)S(1)} collective-permute-done((f32[2,144,128]{2,0,1:T(2,128)S(1)}, f32[2,144,128]{2,0,1:T(2,128)S(1)}, u32[]{:S(2)}, u32[]{:S(2)}) %collective-permute-start.8) | collective-permute-done | bytes 147488 | tf_op jit(solution)/shard_map/ppermute | solution.py:55
  90.2 5.2 %collective-permute-done.9 = bf16[288,128]{1,0:T(8,128)(2,1)S(1)} collective-permute-done((bf16[288,128]{1,0:T(8,128)(2,1)S(1)}, bf16[288,128]{1,0:T(8,128)(2,1)S(1)}, u32[]{:S(2)}, u32[]{:S(2)}) %collective-permute-start.9) | collective-permute-done | bytes 73760 | tf_op jit(solution)/shard_map/ppermute | solution.py:55
  96.5 7.2 %all-to-all-start.3 = ((bf16[8,320,128]{2,1,0:T(8,128)(2,1)}), bf16[8,320,128]{2,1,0:T(8,128)(2,1)}, u32[]{:S(2)}, u32[]{:S(2)}) async-start(bf16[8,320,128]{2,1,0:T(8,128)(2,1)} %fusion.18), calls=%async_computation.3 | async-start | bytes 1310720 | tf_op jit(solution)/shard_map/all_to_all | solution.py:51
  103.7 2.7 %fusion.21 = f32[256,1024]{1,0:T(8,128)S(1)} fusion(bf16[1,256,4608]{2,1,0:T(8,128)(2,1)S(1)} %copy-done, s32[]{:T(128)S(6)} %dynamic_slice.33, bf16[1,1152,1024]{2,1,0:T(8,128)(2,1)} %param.9), kind=kOutput, calls=%fused_computation.33 | convolution fusion | flops 603979776 | bytes 3997700 | tf_op jit(solution)/shard_map/dot_general | solution.py:59
  106.5 1.9 %constant_dynamic-slice_fusion = bf16[256,1152]{1,0:T(8,128)(2,1)} fusion(bf16[256,2304]{1,0:T(8,128)(2,1)} %collective-permute-done.1, s32[]{:T(128)S(6)} %select_n.63), kind=kLoop, calls=%fused_computation.59 | loop fusion | bytes 1179652 | tf_op jit(solution)/shard_map/dynamic_slice | solution.py:119
  108.5 2.7 %fusion.37 = f32[256,1024]{1,0:T(8,128)S(1)} fusion(bf16[256,1152]{1,0:T(8,128)(2,1)} %constant_dynamic-slice_fusion, bf16[1152,1024]{1,0:T(8,128)(2,1)} %collective-permute-done), kind=kOutput, calls=%fused_computation.65 | convolution fusion | flops 603979776 | bytes 3997696 | tf_op jit(solution)/shard_map/dot_general | solution.py:59
  111.2 2.8 %fusion.15 = bf16[256,1024]{1,0:T(8,128)(2,1)} fusion(f32[256,1024]{1,0:T(8,128)S(1)} %fusion.37, bf16[256,2304]{1,0:T(8,128)(2,1)} %collective-permute-done.1, s32[]{:T(128)S(6)} %select_n.58, bf16[1,1152,1024]{2,1,0:T(8,128)(2,1)S(1)} %copy-done.1), kind=kOutput, calls=%fused_computation.25 | convolution fusion | flops 604766208 | bytes 4521988 | tf_op jit(solution)/shard_map/dot_general | solution.py:59
  114.6 8.7 %all-to-all-done.3 = bf16[8,320,128]{2,1,0:T(8,128)(2,1)} async-done(((bf16[8,320,128]{2,1,0:T(8,128)(2,1)}), bf16[8,320,128]{2,1,0:T(8,128)(2,1)}, u32[]{:S(2)}, u32[]{:S(2)}) %all-to-all-start.3) | async-done | bytes 655392 | tf_op jit(solution)/shard_map/all_to_all | solution.py:51
  124.7 1.7 broadcast_in_dim.16
  126.4 4.5 %all-to-all-start.4 = ((bf16[4,8,288,128]{3,1,2,0:T(8,128)(2,1)}), bf16[4,8,288,128]{3,1,2,0:T(8,128)(2,1)}, u32[]{:S(2)}, u32[]{:S(2)}) async-start(bf16[4,8,288,128]{3,1,2,0:T(8,128)(2,1)} %broadcast_in_dim.16), calls=%async_computation.4 | async-start | bytes 4718592 | tf_op jit(solution)/shard_map/all_to_all | solution.py:47
  130.9 3.5 %convolution_add_fusion.2 = f32[1152,1024]{1,0:T(8,128)S(1)} fusion(f32[1152,1024]{1,0:T(8,128)} %fusion.19, bf16[256,1152]{1,0:T(8,128)(2,1)} %collective-permute-done.3, bf16[256,1024]{1,0:T(8,128)(2,1)} %collective-permute-done.4), kind=kOutput, calls=%fused_computation.4 | convolution fusion | flops 605159424 | bytes 10551296 | tf_op jit(solution)/shard_map/dot_general | solution.py:59
  134.7 4.2 %convolution_add_fusion.1 = f32[1152,1024]{1,0:T(8,128)} fusion(f32[1152,1024]{1,0:T(8,128)S(1)} %convolution_add_fusion.2, bf16[256,1024]{1,0:T(8,128)(2,1)} %collective-permute-done.5, bf16[256,2304]{1,0:T(8,128)(2,1)} %collective-permute-done.1, s32[]{:T(128)S(6)} %select_n.58), kind=kOutput, calls=%fused_computation.3 | convolution fusion | flops 605159424 | bytes 10551300 | tf_op jit(solution)/shard_map/dot_general | solution.py:59
  138.9 3.6 %fusion.17 = bf16[1,256,1024]{2,1,0:T(8,128)(2,1)} fusion(f32[256,1024]{1,0:T(8,128)S(1)} %fusion.21, bf16[256,1152]{1,0:T(8,128)(2,1)} %dynamic-slice_bitcast_fusion.1, bf16[1152,1024]{1,0:T(8,128)(2,1)} %collective-permute-done, bf16[256,1024]{1,0:T(8,128)(2,1)} %collective-permute-done.2), kind=kOutput, calls=%fused_computation.27 | convolution fusion | flops 605290496 | bytes 5046272 | tf_op jit(solution)/shard_map/dot_general | solution.py:59
  144.8 15.1 %all-to-all-done.4 = bf16[4,8,288,128]{3,1,2,0:T(8,128)(2,1)} async-done(((bf16[4,8,288,128]{3,1,2,0:T(8,128)(2,1)}), bf16[4,8,288,128]{3,1,2,0:T(8,128)(2,1)}, u32[]{:S(2)}, u32[]{:S(2)}) %all-to-all-start.4) | async-done | bytes 2359328 | tf_op jit(solution)/shard_map/all_to_all | solution.py:47
  159.9 2.1 %convert_element_type.81 = f32[4,8,288,128]{3,1,2,0:T(8,128)S(1)} convert(bf16[4,8,288,128]{3,1,2,0:T(8,128)(2,1)} %all-to-all-done.4) | non-fusion elementwise | flops 1179648 | bytes 7077888 | tf_op jit(solution)/shard_map/convert_element_type | solution.py:145
  163.7 9.5 %fusion.10 = bf16[1,1152,1024]{2,1,0:T(8,128)(2,1)} fusion(f32[144,8,8,128]{3,2,1,0:T(8,128)S(1)} %bitcast.85, bf16[1,1152,1024]{2,1,0:T(8,128)(2,1)} %param.11, f32[1152,1024]{1,0:T(8,128)S(1)} %copy-done.3, bf16[256,1152]{1,0:T(8,128)(2,1)} %collective-permute-done.6, bf16[256,1024]{1,0:T(8,128)(2,1)} %collective-permute-done.7, ...), kind=kOutput, calls=%fused_computation.17 | convolution fusion | flops 631111680 | bytes 19988480 | tf_op jit(solution)/shard_map/dot_general | solution.py:59
  (52 shorter events, 15.7 us)
Async XLA Ops:
  0.6 55.4 %copy-start = (bf16[1,256,4608]{2,1,0:T(8,128)(2,1)S(1)}, bf16[1,256,4608]{2,1,0:T(8,128)(2,1)}, u32[]{:S(2)}) copy-start(bf16[1,256,4608]{2,1,0:T(8,128)(2,1)} %param.7) | copy-start | bytes 7077892
  0.6 4.7 %copy-start.4 = (f32[1,18,1024]{2,0,1:T(1,128)S(1)}, f32[1,18,1024]{2,0,1:T(1,128)}, u32[]{:S(2)}) copy-start(f32[1,18,1024]{2,0,1:T(1,128)} %param.13) | copy-start | bytes 221188
  0.7 4.7 %copy-start.5 = (f32[1,18,1024]{2,0,1:T(1,128)S(1)}, f32[1,18,1024]{2,0,1:T(1,128)}, u32[]{:S(2)}) copy-start(f32[1,18,1024]{2,0,1:T(1,128)} %param.12) | copy-start | bytes 221188
  0.7 34.1 %all-to-all-start.1 = ((bf16[4,288,1024]{2,1,0:T(8,128)(2,1)}), bf16[4,288,1024]{2,1,0:T(8,128)(2,1)}, u32[]{:S(2)}, u32[]{:S(2)}) async-start(bf16[4,288,1024]{2,1,0:T(8,128)(2,1)} %bitcast.83), calls=%async_computation.1 | async-start | bytes 4718592 | tf_op jit(solution)/shard_map/all_to_all | solution.py:47
  34.8 16.4 %all-to-all-start = ((f32[8,2,18,128]{3,1,2,0:T(2,128)}), f32[8,2,18,128]{3,1,2,0:T(2,128)S(1)}, u32[]{:S(2)}, u32[]{:S(2)}) async-start(f32[8,2,18,128]{3,1,2,0:T(2,128)} %bitcast_bitcast_fusion), calls=%async_computation | async-start | bytes 294912 | tf_op jit(solution)/shard_map/all_to_all | solution.py:51
  43.4 87.5 %collective-permute-start.4 = (bf16[256,1024]{1,0:T(8,128)(2,1)}, bf16[256,1024]{1,0:T(8,128)(2,1)}, u32[]{:S(2)}, u32[]{:S(2)}) collective-permute-start(bf16[256,1024]{1,0:T(8,128)(2,1)} %bitcast.6), channel_id=1, source_target_pairs={{0,1},{1,0},{2,3},{3,2},{4,5},{5,4},{6,7},{7,6},{8,9},{9,8},{10,11... | collective-permute-start | bytes 1572872 | tf_op jit(solution)/shard_map/ppermute | solution.py:55
  43.4 63.0 %collective-permute-start.5 = (bf16[256,1024]{1,0:T(8,128)(2,1)}, bf16[256,1024]{1,0:T(8,128)(2,1)}, u32[]{:S(2)}, u32[]{:S(2)}) collective-permute-start(bf16[256,1024]{1,0:T(8,128)(2,1)} %bitcast.6), channel_id=1, source_target_pairs={{0,2},{1,3},{2,0},{3,1},{4,6},{5,7},{6,4},{7,5},{8,10},{9,11},{10,... | collective-permute-start | bytes 1572872 | tf_op jit(solution)/shard_map/ppermute | solution.py:55
  45.0 63.5 %collective-permute-start = (bf16[1152,1024]{1,0:T(8,128)(2,1)}, bf16[1152,1024]{1,0:T(8,128)(2,1)}, u32[]{:S(2)}, u32[]{:S(2)}) collective-permute-start(bf16[1152,1024]{1,0:T(8,128)(2,1)} %bitcast.84), channel_id=1, source_target_pairs={{0,1},{1,0},{2,3},{3,2},{4,5},{5,4},{6,7},{7,6},{8,9},{9,8},{10,11... | collective-permute-start | bytes 7077896 | tf_op jit(solution)/shard_map/ppermute | solution.py:55
  51.2 38.2 %all-to-all-start.2 = ((bf16[8,288,128]{2,1,0:T(8,128)(2,1)}), bf16[8,288,128]{2,1,0:T(8,128)(2,1)S(1)}, u32[]{:S(2)}, u32[]{:S(2)}) async-start(bf16[8,288,128]{2,1,0:T(8,128)(2,1)} %copy.19), calls=%async_computation.2 | async-start | bytes 1179648 | tf_op jit(solution)/shard_map/all_to_all | solution.py:51
  57.2 49.4 %collective-permute-start.1 = (bf16[256,2304]{1,0:T(8,128)(2,1)}, bf16[256,2304]{1,0:T(8,128)(2,1)}, u32[]{:S(2)}, u32[]{:S(2)}) collective-permute-start(bf16[256,2304]{1,0:T(8,128)(2,1)} %dynamic-slice_bitcast_fusion), channel_id=1, source_target_pairs={{0,2},{1,3},{2,0},{3,1},{4,6},{5,7},{6,4},{7,5},{8,10},{9,11},{10,... | collective-permute-start | bytes 3538952 | tf_op jit(solution)/shard_map/ppermute | solution.py:55
  63.0 26.3 %collective-permute-start.8 = (f32[2,144,128]{2,0,1:T(2,128)S(1)}, f32[2,144,128]{2,0,1:T(2,128)S(1)}, u32[]{:S(2)}, u32[]{:S(2)}) collective-permute-start(f32[2,144,128]{2,0,1:T(2,128)S(1)} %bitcast.88), channel_id=1, source_target_pairs={{0,32},{1,33},{2,34},{3,35},{4,36},{5,37},{6,38},{7,39},{8,40},{9,... | collective-permute-start | bytes 442376 | tf_op jit(solution)/shard_map/ppermute | solution.py:55
  89.5 5.9 %collective-permute-start.9 = (bf16[288,128]{1,0:T(8,128)(2,1)S(1)}, bf16[288,128]{1,0:T(8,128)(2,1)S(1)}, u32[]{:S(2)}, u32[]{:S(2)}) collective-permute-start(bf16[288,128]{1,0:T(8,128)(2,1)S(1)} %convert_element_type.71), channel_id=1, source_target_pairs={{0,32},{1,33},{2,34},{3,35},{4,36},{5,37},{6,38},{7,39},{8,40},{9,... | collective-permute-start | bytes 221192 | tf_op jit(solution)/shard_map/ppermute | solution.py:55
  95.4 35.5 %collective-permute-start.3 = (bf16[256,1152]{1,0:T(8,128)(2,1)}, bf16[256,1152]{1,0:T(8,128)(2,1)}, u32[]{:S(2)}, u32[]{:S(2)}) collective-permute-start(bf16[256,1152]{1,0:T(8,128)(2,1)} %dynamic-slice_bitcast_fusion.1), channel_id=1, source_target_pairs={{0,1},{1,0},{2,3},{3,2},{4,5},{5,4},{6,7},{7,6},{8,9},{9,8},{10,11... | collective-permute-start | bytes 1769480 | tf_op jit(solution)/shard_map/ppermute | solution.py:55
  96.5 26.8 %all-to-all-start.3 = ((bf16[8,320,128]{2,1,0:T(8,128)(2,1)}), bf16[8,320,128]{2,1,0:T(8,128)(2,1)}, u32[]{:S(2)}, u32[]{:S(2)}) async-start(bf16[8,320,128]{2,1,0:T(8,128)(2,1)} %fusion.18), calls=%async_computation.3 | async-start | bytes 1310720 | tf_op jit(solution)/shard_map/all_to_all | solution.py:51
  103.7 7.5 %copy-start.1 = (bf16[1,1152,1024]{2,1,0:T(8,128)(2,1)S(1)}, bf16[1,1152,1024]{2,1,0:T(8,128)(2,1)}, u32[]{:S(2)}) copy-start(bf16[1,1152,1024]{2,1,0:T(8,128)(2,1)} %param.9) | copy-start | bytes 7077892
  106.4 55.6 %collective-permute-start.7 = (bf16[256,1024]{1,0:T(8,128)(2,1)}, bf16[256,1024]{1,0:T(8,128)(2,1)}, u32[]{:S(2)}, u32[]{:S(2)}) collective-permute-start(bf16[256,1024]{1,0:T(8,128)(2,1)} %collective-permute-done.5), channel_id=1, source_target_pairs={{0,1},{1,0},{2,3},{3,2},{4,5},{5,4},{6,7},{7,6},{8,9},{9,8},{10,11... | collective-permute-start | bytes 1572872 | tf_op jit(solution)/shard_map/ppermute | solution.py:55
  113.9 24.9 %collective-permute-start.2 = (bf16[256,1024]{1,0:T(8,128)(2,1)}, bf16[256,1024]{1,0:T(8,128)(2,1)}, u32[]{:S(2)}, u32[]{:S(2)}) collective-permute-start(bf16[256,1024]{1,0:T(8,128)(2,1)} %fusion.15), channel_id=1, source_target_pairs={{0,2},{1,3},{2,0},{3,1},{4,6},{5,7},{6,4},{7,5},{8,10},{9,11},{10,... | collective-permute-start | bytes 1572872 | tf_op jit(solution)/shard_map/ppermute | solution.py:55
  126.4 33.6 %all-to-all-start.4 = ((bf16[4,8,288,128]{3,1,2,0:T(8,128)(2,1)}), bf16[4,8,288,128]{3,1,2,0:T(8,128)(2,1)}, u32[]{:S(2)}, u32[]{:S(2)}) async-start(bf16[4,8,288,128]{3,1,2,0:T(8,128)(2,1)} %broadcast_in_dim.16), calls=%async_computation.4 | async-start | bytes 4718592 | tf_op jit(solution)/shard_map/all_to_all | solution.py:47
  134.4 27.7 %collective-permute-start.6 = (bf16[256,1152]{1,0:T(8,128)(2,1)}, bf16[256,1152]{1,0:T(8,128)(2,1)}, u32[]{:S(2)}, u32[]{:S(2)}) collective-permute-start(bf16[256,1152]{1,0:T(8,128)(2,1)} %constant_dynamic-slice_fusion), channel_id=1, source_target_pairs={{0,1},{1,0},{2,3},{3,2},{4,5},{5,4},{6,7},{7,6},{8,9},{9,8},{10,11... | collective-permute-start | bytes 1769480 | tf_op jit(solution)/shard_map/ppermute | solution.py:55
  159.9 2.4 %copy-start.2 = (bf16[1,1152,1024]{2,1,0:T(8,128)(2,1)S(1)}, bf16[1,1152,1024]{2,1,0:T(8,128)(2,1)}, u32[]{:S(2)}) copy-start(bf16[1,1152,1024]{2,1,0:T(8,128)(2,1)} %param.9) | copy-start | bytes 7077892
  159.9 3.8 %copy-start.3 = (f32[1152,1024]{1,0:T(8,128)S(1)}, f32[1152,1024]{1,0:T(8,128)}, u32[]{:S(2)}) copy-start(f32[1152,1024]{1,0:T(8,128)} %convolution_add_fusion.1) | copy-start | bytes 14155780

commit v2 on v1

v2 whole, which is shorter than its diff:
```python
import jax
import jax.numpy as jnp
from jax import lax
from jax.experimental import pallas as pl
from jax.experimental.pallas import tpu as pltpu
from jax.sharding import PartitionSpec as P

beta_one = 0.9
beta_two = 0.95
bias_one = 1.0 - 0.9**8
bias_two = 1.0 - 0.95**8
inner_rate = 0.25
decay_rate = 0.1
epsilon = 1e-08
outer_rate = 0.7
outer_mu = 0.9
mixing = 0.5

NX, NYH, NZ = 4, 2, 8
NYL, NC = 2, 2
BOTH = ("rep", "fsdp")
PLANE = NYH * NZ
HZ_GROUPS = [[x * PLANE + k for k in range(PLANE)] for x in range(NX)]
Z_GROUPS = [[(x * NYH + h) * NZ + z for z in range(NZ)] for x in range(NX) for h in range(NYH)]


def pairs(move):
    found = []
    for x in range(NX):
        for h in range(NYH):
            for z in range(NZ):
                for y in range(NYL):
                    for c in range(NC):
                        x2, y2, c2 = move(x, y, c)
                        found.append(
                            (
                                ((x * NYH + h) * NZ + z) * 4 + y * 2 + c,
                                ((x2 * NYH + h) * NZ + z) * 4 + y2 * 2 + c2,
                            )
                        )
    return found


TO_OTHER_CORE = pairs(lambda x, y, c: (x, y, 1 - c))
TO_OTHER_CHIP = pairs(lambda x, y, c: (x, 1 - y, c))
TO_X = [pairs(lambda x, y, c, d=d: ((x + d) % NX, y, c)) for d in range(NX)]

MIB = 1024 * 1024
BF16, F32 = jnp.bfloat16, jnp.float32


def over(array, groups):
    return lax.all_to_all(array, "rep", 0, 0, axis_index_groups=groups)


def swap(array, to):
    return lax.ppermute(array, BOTH, to)


def dot(a, b):
    return jnp.dot(a, b, preferred_element_type=F32)


def dot_t(a, b):
    return lax.dot_general(a, b, (((0,), (0,)), ((), ())), preferred_element_type=F32)


def inside(array):
    return pltpu.with_memory_space_constraint(array, pltpu.VMEM)


def outside(array):
    return pltpu.with_memory_space_constraint(array, pltpu.HBM)


def call(kernel, grid, in_specs, out_specs, out_shape, flops, moved, at, *operands):
    spec = pltpu.PrefetchScalarGridSpec(
        num_scalar_prefetch=1, grid=grid, in_specs=in_specs, out_specs=out_specs
    )
    return pl.pallas_call(
        kernel,
        grid_spec=spec,
        out_shape=out_shape,
        compiler_params=pltpu.CompilerParams(vmem_limit_bytes=48 * MIB),
        cost_estimate=pl.CostEstimate(flops=flops, bytes_accessed=moved, transcendentals=0),
    )(at, *operands)


def copy_out(places, array, shapes, at, after=()):
    count = len(shapes)

    def kernel(at_ref, x_ref, *rest):
        outs = rest[len(after) : len(after) + count]
        *held, in_sems, out_sems = rest[len(after) + count :]
        ins = [
            pltpu.make_async_copy(x_ref.at[place], held[k], in_sems.at[k])
            for k, place in enumerate(places(at_ref))
        ]
        backs = [pltpu.make_async_copy(held[k], outs[k], out_sems.at[k]) for k in range(count)]
        for copy in ins:
            copy.start()
        for copy, back in zip(ins, backs, strict=True):
            copy.wait()
            back.start()
        for back in backs:
            back.wait()

    hbm = pl.BlockSpec(memory_space=pl.ANY)
    size = sum(x[0] * x[1] for x in shapes)
    return pl.pallas_call(
        kernel,
        in_specs=[pl.BlockSpec(memory_space=pltpu.SMEM), hbm] + [hbm] * len(after),
        out_specs=[hbm] * count,
        out_shape=[pltpu.HBM(x, BF16) for x in shapes],
        scratch_shapes=[pltpu.VMEM(x, BF16) for x in shapes]
        + [pltpu.SemaphoreType.DMA((count,)), pltpu.SemaphoreType.DMA((count,))],
        compiler_params=pltpu.CompilerParams(vmem_limit_bytes=8 * MIB),
        cost_estimate=pl.CostEstimate(flops=0, bytes_accessed=4 * size, transcendentals=0),
    )(at, outside(array), *after)


def cut_weights(at, w):
    block = w.shape[0] // NX

    def places(at_ref):
        bases = [lax.rem(at_ref[0] + d, NX) * block for d in range(1, NX)]
        return [(pl.ds(pl.multiple_of(base, 16), block), slice(None)) for base in bases]

    return copy_out(places, w, [(block, w.shape[1])] * (NX - 1), at)


def cut_hidden(at, h, after):
    toks, width = h.shape
    chip, rows = width // NYL, width // (NYL * NC)

    def places(at_ref):
        far, near = (1 - at_ref[5]) * chip, at_ref[3] * rows
        return [
            (slice(None), pl.ds(pl.multiple_of(far, 128), chip)),
            (slice(None), pl.ds(pl.multiple_of(near, 128), rows)),
        ]

    return copy_out(places, h, [(toks, chip), (toks, rows)], at, [after])


def sum_over_x(blocks, after):
    block, cols = blocks[0].shape
    half, lane = block // NYH, cols // NZ

    def kernel(w_ref, a_ref, b_ref, c_ref, after_ref, o_ref, held, sems):
        copies = []
        for i in range(NYH):
            rows = pl.ds(i * half, half)
            for z in range(NZ):
                at_z = (rows, pl.ds(z * lane, lane))
                total = w_ref[at_z].astype(F32) + a_ref[at_z].astype(F32)
                total = total + (b_ref[at_z].astype(F32) + c_ref[at_z].astype(F32))
                held[i, z] = total.astype(BF16)
            copies.append(pltpu.make_async_copy(held.at[i], o_ref.at[i], sems.at[i]))
            copies[-1].start()
        for copy in copies:
            copy.wait()

    shape = (NYH, NZ, half, lane)
    return pl.pallas_call(
        kernel,
        in_specs=[pl.BlockSpec(memory_space=pltpu.VMEM)] * NX + [pl.BlockSpec(memory_space=pl.ANY)],
        out_specs=pl.BlockSpec(memory_space=pl.ANY),
        out_shape=pltpu.HBM(shape, BF16),
        scratch_shapes=[pltpu.VMEM(shape, BF16), pltpu.SemaphoreType.DMA((NYH,))],
        compiler_params=pltpu.CompilerParams(vmem_limit_bytes=8 * MIB),
        cost_estimate=pl.CostEstimate(flops=3 * block * cols, bytes_accessed=10 * block * cols, transcendentals=0),
    )(*[inside(x) for x in blocks], after)


def outer_step(parts, state, replicas, *after):
    plane = parts.shape[0]

    def kernel(p_ref, s_ref, *rest):
        r_ref, o_ref, held, sems = rest[-4:]
        summed = p_ref[0].astype(F32)
        for k in range(1, plane):
            summed = summed + p_ref[k].astype(F32)
        pseudo = s_ref[0] - summed / replicas
        momentum = outer_mu * s_ref[1] + pseudo
        renewed = s_ref[0] - outer_rate * (pseudo + outer_mu * momentum)
        held[...] = renewed.astype(BF16)
        copies = [pltpu.make_async_copy(held, r_ref.at[k], sems.at[k]) for k in range(plane)]
        for copy in copies:
            copy.start()
        o_ref[0] = renewed
        o_ref[1] = momentum
        for copy in copies:
            copy.wait()

    vmem = pl.BlockSpec(memory_space=pltpu.VMEM)
    hbm = pl.BlockSpec(memory_space=pl.ANY)
    return pl.pallas_call(
        kernel,
        in_specs=[vmem, vmem] + [hbm] * len(after),
        out_specs=[hbm, vmem],
        out_shape=[pltpu.HBM(parts.shape, BF16), pltpu.HBM(state.shape, F32)],
        scratch_shapes=[pltpu.VMEM(parts.shape[1:], BF16), pltpu.SemaphoreType.DMA((plane,))],
        compiler_params=pltpu.CompilerParams(vmem_limit_bytes=8 * MIB),
        cost_estimate=pl.CostEstimate(flops=2 * parts.size, bytes_accessed=4 * parts.size, transcendentals=0),
    )(inside(parts), inside(state), *after)


def project(at, got, hidden, w, w_other, factor, after):
    rows, cols = w.shape
    toks = got.shape[0]
    steps = 4
    wide = cols // steps

    def kernel(at_ref, a_ref, b_ref, c_ref, d_ref, w_ref, v_ref, after_ref, far_ref, near_ref):
        far_ref[...] = ((dot(a_ref[...], w_ref[...]) + dot(b_ref[...], v_ref[...])) * factor).astype(BF16)
        near_ref[...] = (dot(c_ref[...], w_ref[...]) + dot(d_ref[...], v_ref[...])) * factor

    def left(k):
        return pl.BlockSpec((toks, rows), lambda i, at: (0, at[k]))

    column = pl.BlockSpec((toks, wide), lambda i, at: (0, i))
    wspec = pl.BlockSpec((rows, wide), lambda i, at: (0, i))
    return call(
        kernel,
        (steps,),
        [left(2), left(4), left(1), left(3), wspec, wspec, pl.BlockSpec(memory_space=pl.ANY)],
        [column, column],
        [jax.ShapeDtypeStruct((toks, cols), BF16), jax.ShapeDtypeStruct((toks, cols), F32)],
        8 * toks * rows * cols,
        4 * rows * cols + 8 * toks * rows,
        at,
        got,
        got,
        outside(hidden),
        outside(hidden),
        outside(w),
        outside(w_other),
        after,
    )


def hold(array, *after):
    hbm = pl.BlockSpec(memory_space=pl.ANY)
    return pl.pallas_call(
        lambda *refs: None,
        in_specs=[hbm] * (1 + len(after)),
        out_specs=hbm,
        out_shape=jax.ShapeDtypeStruct(array.shape, array.dtype),
        input_output_aliases={0: 0},
        compiler_params=pltpu.CompilerParams(vmem_limit_bytes=MIB),
    )(array, *after)


def finish(near, far, outer):
    def kernel(n_ref, f_ref, outer_ref, o_ref, out_ref):
        o_ref[...] = (n_ref[...] + f_ref[...].astype(F32)).astype(BF16)

    vmem, hbm = pl.BlockSpec(memory_space=pltpu.VMEM), pl.BlockSpec(memory_space=pl.ANY)
    return pl.pallas_call(
        kernel,
        in_specs=[vmem, vmem, hbm],
        out_specs=[vmem, hbm],
        out_shape=[jax.ShapeDtypeStruct(near.shape, BF16), pltpu.HBM(outer.shape, F32)],
        input_output_aliases={2: 1},
        compiler_params=pltpu.CompilerParams(vmem_limit_bytes=16 * MIB),
        cost_estimate=pl.CostEstimate(flops=near.size, bytes_accessed=8 * near.size, transcendentals=0),
    )(near, far, outside(outer))


def inner_step(at, hidden, near, far_got, far, upstreams, w, m1, m2, factor, after):
    rows, cols = w.shape
    toks = hidden.shape[0]
    tall = 384
    steps = rows // tall

    def kernel(at_ref, h_ref, n_ref, g_ref, f_ref, hu_ref, nu_ref, gu_ref, fu_ref, w_ref, m1_ref, m2_ref, after_ref, o_ref):
        gradient = dot_t(h_ref[...], hu_ref[...]) + dot_t(n_ref[...], nu_ref[...])
        gradient = gradient + dot_t(g_ref[...], gu_ref[...]) + dot_t(f_ref[...], fu_ref[...])
        gradient = gradient * factor
        moment_new = beta_one * m1_ref[...].astype(F32) + (1.0 - beta_one) * gradient
        second_new = beta_two * m2_ref[...].astype(F32) + (1.0 - beta_two) * gradient * gradient
        scale = jnp.sqrt(second_new * (1.0 / bias_two)) + epsilon
        stepped = moment_new * (mixing * inner_rate / bias_one) / scale
        o_ref[...] = (mixing * (1.0 - inner_rate * decay_rate)) * w_ref[...].astype(F32) - stepped

    def left(first):
        return pl.BlockSpec((toks, tall), first)

    whole = pl.BlockSpec((toks, cols), lambda i, at: (0, 0))
    own = pl.BlockSpec((tall, cols), lambda i, at: (i, 0))
    spec = pltpu.PrefetchScalarGridSpec(
        num_scalar_prefetch=1,
        grid=(steps,),
        in_specs=[
            left(lambda i, at: (0, at[1] * steps + i)),
            left(lambda i, at: (0, i)),
            left(lambda i, at: (0, at[2] * steps + i)),
            left(lambda i, at: (0, i)),
            whole,
            whole,
            whole,
            whole,
            own,
            own,
            own,
            pl.BlockSpec(memory_space=pl.ANY),
        ],
        out_specs=own,
    )
    operands = [outside(hidden), near, far_got, far] + upstreams + [outside(w), outside(m1), outside(m2), after]
    return pl.pallas_call(
        kernel,
        grid_spec=spec,
        out_shape=pltpu.HBM((rows, cols), F32),
        compiler_params=pltpu.CompilerParams(vmem_limit_bytes=40 * MIB),
        cost_estimate=pl.CostEstimate(
            flops=8 * toks * rows * cols, bytes_accessed=10 * rows * cols, transcendentals=0
        ),
    )(at, *operands)


def merge(at, kept, spread):
    rows, cols = kept.shape
    plane, half, lane = spread[0].shape
    nz = plane // NYH
    block = NYH * half

    def kernel(at_ref, k_ref, a_ref, b_ref, c_ref, d_ref, o_ref, kept_ref, held, in_sems, out_sems):
        refs = [a_ref, b_ref, c_ref, d_ref]
        places = [pl.ds(pl.multiple_of(lax.rem(at_ref[0] + NX - d, NX) * block, 16), block) for d in range(NX)]
        ins = [pltpu.make_async_copy(k_ref.at[places[d]], kept_ref.at[d], in_sems.at[d]) for d in range(NX)]
        outs = [pltpu.make_async_copy(held.at[d], o_ref.at[places[d]], out_sems.at[d]) for d in range(NX)]
        for copy in ins:
            copy.start()
        for d in range(NX):
            ins[d].wait()
            for i in range(NYH):
                for z in range(nz):
                    at_z = (d, pl.ds(i * half, half), pl.ds(z * lane, lane))
                    new = (1.0 - mixing) * refs[d][i * nz + z].astype(F32)
                    held[at_z] = (kept_ref[at_z] + new).astype(BF16)
            outs[d].start()
        for copy in outs:
            copy.wait()

    vmem, hbm = pl.BlockSpec(memory_space=pltpu.VMEM), pl.BlockSpec(memory_space=pl.ANY)
    return pl.pallas_call(
        kernel,
        in_specs=[pl.BlockSpec(memory_space=pltpu.SMEM), hbm] + [vmem] * NX,
        out_specs=hbm,
        out_shape=jax.ShapeDtypeStruct((rows, cols), BF16),
        scratch_shapes=[
            pltpu.VMEM((NX, block, cols), F32),
            pltpu.VMEM((NX, block, cols), BF16),
            pltpu.SemaphoreType.DMA((NX,)),
            pltpu.SemaphoreType.DMA((NX,)),
        ],
        compiler_params=pltpu.CompilerParams(vmem_limit_bytes=24 * MIB),
        cost_estimate=pl.CostEstimate(flops=2 * rows * cols, bytes_accessed=8 * rows * cols, transcendentals=0),
    )(at, outside(kept), *[inside(x) for x in spread])


def on_device(hidden, upstream, weights, moment_one, moment_two, global_params, outer_momentum):
    width = hidden.shape[2]
    rows, cols = weights.shape[1:]
    factor = float(width) ** (-0.5)
    own_rows = global_params.shape[1]
    block = rows // NX
    lane = cols // NZ
    half = block // NYH
    rep, fsdp = lax.axis_index("rep"), lax.axis_index("fsdp")
    core, pair = fsdp % NC, fsdp // NC
    x_at = rep // PLANE
    sibling = pair * NC + 1 - core
    at = jnp.stack([x_at, fsdp, core, sibling, 1 - core, pair]).astype(jnp.int32)

    w, h, u = weights[0], hidden[0], upstream[0]

    sent = cut_weights(at, w)
    got = [swap(x, TO_X[d]) for d, x in enumerate(sent, 1)]

    h_sent, h_near = cut_hidden(at, h, sent[0])
    h_got = swap(h_sent, TO_OTHER_CHIP)
    u_got = swap(u, TO_OTHER_CHIP)
    w_other = swap(w, TO_OTHER_CORE)
    h_near = swap(h_near, TO_OTHER_CORE)
    u_near = swap(u, TO_OTHER_CORE)
    h_far = swap(lax.dynamic_slice_in_dim(h_got, (1 - core) * rows, rows, 1), TO_OTHER_CORE)

    state = jnp.stack([global_params[0], outer_momentum[0]]).reshape(2, own_rows, NZ, lane)
    state = over(state.transpose(2, 0, 1, 3), Z_GROUPS)
    state = state.transpose(1, 0, 2, 3).reshape(2, half, lane)

    own = lax.dynamic_slice_in_dim(w, x_at * block, block, 0)
    sum_x = sum_over_x([own] + got, h_got)
    parts = over(sum_x.reshape(PLANE, half, lane), HZ_GROUPS)
    far_sent, near = project(at, h_got, h, w, w_other, factor, sum_x)
    u_got = hold(u_got, far_sent)
    u_far = swap(u_got, TO_OTHER_CORE)
    renewed, outer = outer_step(parts, state, lax.axis_size("rep"), u_got)
    upstreams = [u, u_near, u_got, u_far]
    kept = inner_step(
        at, h, h_near, h_got, h_far, upstreams, w, moment_one[0], moment_two[0], factor, renewed
    )
    spread = [over(renewed, HZ_GROUPS)]
    for d in range(1, NX):
        spread.append(swap(spread[0], TO_X[d]))

    values, outer = finish(near, swap(far_sent, TO_OTHER_CHIP), outer)
    outer = outer.reshape(2, NZ, own_rows, lane).transpose(1, 0, 2, 3)
    outer = over(outer, Z_GROUPS).transpose(1, 2, 0, 3).reshape(2, own_rows, cols)
    merged = merge(at, kept, spread)
    return (values[None], merged[None], outer[0][None], outer[1][None])


def solution(mesh):
    return jax.shard_map(
        on_device,
        mesh=mesh,
        in_specs=(
            P("rep", "fsdp", None),
            P("rep", "fsdp", None),
            P("rep", "fsdp", None),
            P("rep", "fsdp", None),
            P("rep", "fsdp", None),
            P("fsdp", "rep", None),
            P("fsdp", "rep", None),
        ),
        out_specs=(
            P("rep", "fsdp", None),
            P("rep", "fsdp", None),
            P("fsdp", "rep", None),
            P("fsdp", "rep", None),
        ),
        check_vma=False,
    )
```

time: 176 us -> 135 us (0.77)
  waiting for transfers between devices: 82.8 us -> 39.3 us
  matrix products: 33.2 us -> 0 us
  Pallas kernels: 0 us -> 32.4 us
  starting transfers between devices: 37.6 us -> 50 us
  other arithmetic: 7.37 us -> 0.8 us
    all_to_all x5 -> x4, waiting for transfers between devices: 55.3 us -> 14.6 us  [over(): return lax.all_to_all(array, 'rep', 0, 0, axis_index_groups=groups)]
    dot_general x8 -> x0, matrix products: 33.2 us -> none  [dot(): lax.dot_general(a, b, (contract, ((), ())), preferred_element_type=jnp.fl...]
    pallas_call x0 -> x9, Pallas kernels: none -> 32.4 us  [the longest x1 10.6 us: inner_step(): pl.pallas_call(kernel, grid_spec=spec, out_shape=pltpu.HBM((rows, cols),...]
    ppermute x10 -> x14, starting transfers between devices: 7.77 us -> 14.8 us  [swap(): return lax.ppermute(array, BOTH, to)]
    all_to_all x5 -> x4, starting transfers between devices: 29.8 us -> 35.2 us  [over(): return lax.all_to_all(array, 'rep', 0, 0, axis_index_groups=groups)]
    ppermute x10 -> x14, waiting for transfers between devices: 27.5 us -> 24.6 us  [swap(): return lax.ppermute(array, BOTH, to)]
    reduce_sum x2 -> x0, other arithmetic: 2.23 us -> none  [the longest x1 2.15 us: on_device(): sum_x = jnp.sum(parts_x.astype(f32), axis=0).astype(bf16)]
    convert_element_type x3 -> x0, other arithmetic: 2.19 us -> none  [the longest x1 2.12 us: on_device(): spread.astype(f32)]
  transfers between devices with their start and end apart: 15 -> 18, of which waited for: 6 -> 4; matrix products, arithmetic and copies ran while one was open for 24% -> 5% of each run, Pallas kernels for 0% -> 19%
where the time goes in v2:
time: 135 us; the launch traced here: 134 us
  starting transfers between devices  50 us (37%)
  waiting for transfers between devices  39.3 us (29%)
  Pallas kernels  32.4 us (24%)
  local copies, waits for them, and re-layouts  10.2 us (8%)
    all_to_all x4, starting transfers between devices, over(): return lax.all_to_all(array, 'rep', 0, 0, axis_index_groups=groups)  35.2 us
    ppermute x14, waiting for transfers between devices, swap(): return lax.ppermute(array, BOTH, to)  24.6 us
    ppermute x14, starting transfers between devices, swap(): return lax.ppermute(array, BOTH, to)  14.8 us
    all_to_all x4, waiting for transfers between devices, over(): return lax.all_to_all(array, 'rep', 0, 0, axis_index_groups=groups)  14.6 us
    pallas_call x1, Pallas kernels, inner_step(): pl.pallas_call(kernel, grid_spec=spec, out_shape=pltpu.HBM((rows, cols),...  10.6 us
    pallas_call x1, Pallas kernels, call(): pl.pallas_call(kernel, grid_spec=spec, out_shape=out_shape, compiler_para...  6.27 us
    pallas_call x2, Pallas kernels, copy_out(): pl.pallas_call(kernel, in_specs=[pl.BlockSpec(memory_space=pltpu.SMEM), h...  5.98 us
    pallas_call x1, Pallas kernels, merge(): pl.pallas_call(kernel, in_specs=[pl.BlockSpec(memory_space=pltpu.SMEM), h...  4.84 us
  transfers between devices with their start and end apart: 18, of which 4 were waited for; matrix products, arithmetic and copies ran while one was open for 5% of the time, Pallas kernels for 19%

profile of v2, /device:TPU:32, one launch (start us, length us, event | category | flops | bytes accessed | tf_op | source)
XLA Modules:
  0.0 133.7 jit_solution(8166116675196566016)
XLA Ops:
  0.9 2.9 %shard_map.102 = (bf16[288,1024]{1,0:T(8,128)(2,1)}, bf16[288,1024]{1,0:T(8,128)(2,1)}, bf16[288,1024]{1,0:T(8,128)(2,1)}) custom-call(s32[6]{0:T(128)S(1)} %stack.30.at_ref, bf16[1152,1024]{1,0:T(8,128)(2,1)} %bitcast.38), custom_call_target="tpu_custom_call" | custom-call | bytes 3538944 | tf_op jit(solution)/shard_map/pallas_call | solution.py:110
  3.8 3.1 %shard_map.103 = (bf16[256,2304]{1,0:T(8,128)(2,1)}, bf16[256,1152]{1,0:T(8,128)(2,1)}) custom-call(s32[6]{0:T(128)S(1)} %stack.30.at_ref, bf16[256,4608]{1,0:T(8,128)(2,1)} %bitcast.33, bf16[288,1024]{1,0:T(8,128)(2,1)} %get-tuple-element.15.rest_0_), custom_call_target="tpu_custom_call" | custom-call | bytes 3538944 | tf_op jit(solution)/shard_map/pallas_call | solution.py:110
  6.9 1.7 %collective-permute-start = (bf16[256,2304]{1,0:T(8,128)(2,1)}, bf16[256,2304]{1,0:T(8,128)(2,1)S(1)}, u32[]{:S(2)}, u32[]{:S(2)}) collective-permute-start(bf16[256,2304]{1,0:T(8,128)(2,1)} %get-tuple-element.16), channel_id=1, source_target_pairs={{0,2},{1,3},{2,0},{3,1},{4,6},{5,7},{6,4},{7,5},{8,10},{9,11},{10,... | collective-permute-start | bytes 3538952 | tf_op jit(solution)/shard_map/ppermute | solution.py:57
  8.5 1.5 %collective-permute-start.2 = (bf16[288,1024]{1,0:T(8,128)(2,1)}, bf16[288,1024]{1,0:T(8,128)(2,1)S(1)}, u32[]{:S(2)}, u32[]{:S(2)}) collective-permute-start(bf16[288,1024]{1,0:T(8,128)(2,1)} %get-tuple-element.15.rest_0_), channel_id=1, source_target_pairs={{0,64},{1,65},{2,66},{3,67},{4,68},{5,69},{6,70},{7,71},{8,72},{9,... | collective-permute-start | bytes 1769480 | tf_op jit(solution)/shard_map/ppermute | solution.py:57
  10.0 2.7 %collective-permute-start.3 = (bf16[288,1024]{1,0:T(8,128)(2,1)}, bf16[288,1024]{1,0:T(8,128)(2,1)S(1)}, u32[]{:S(2)}, u32[]{:S(2)}) collective-permute-start(bf16[288,1024]{1,0:T(8,128)(2,1)} %get-tuple-element.17), channel_id=1, source_target_pairs={{0,128},{1,129},{2,130},{3,131},{4,132},{5,133},{6,134},{7,135},{8... | collective-permute-start | bytes 1769480 | tf_op jit(solution)/shard_map/ppermute | solution.py:57
  12.7 1.4 %collective-permute-start.4 = (bf16[288,1024]{1,0:T(8,128)(2,1)}, bf16[288,1024]{1,0:T(8,128)(2,1)S(1)}, u32[]{:S(2)}, u32[]{:S(2)}) collective-permute-start(bf16[288,1024]{1,0:T(8,128)(2,1)} %get-tuple-element.18), channel_id=1, source_target_pairs={{0,192},{1,193},{2,194},{3,195},{4,196},{5,197},{6,198},{7,199},{8... | collective-permute-start | bytes 1769480 | tf_op jit(solution)/shard_map/ppermute | solution.py:57
  15.0 8.6 %all-to-all-start.1 = ((f32[8,2,18,128]{3,1,2,0:T(2,128)}), f32[8,2,18,128]{3,1,2,0:T(2,128)S(1)}, u32[]{:S(2)}, u32[]{:S(2)}) async-start(f32[8,2,18,128]{3,1,2,0:T(2,128)} %bitcast_bitcast_fusion), calls=%async_computation.1 | async-start | bytes 294912 | tf_op jit(solution)/shard_map/all_to_all | solution.py:53
  25.4 13.6 %collective-permute-done.3.b_ref = bf16[288,1024]{1,0:T(8,128)(2,1)S(1)} collective-permute-done((bf16[288,1024]{1,0:T(8,128)(2,1)}, bf16[288,1024]{1,0:T(8,128)(2,1)S(1)}, u32[]{:S(2)}, u32[]{:S(2)}) %collective-permute-start.3) | collective-permute-done | bytes 589856 | tf_op jit(solution)/shard_map/ppermute | solution.py:57
  39.0 1.1 shard_map.104.after_ref
  40.1 10.9 %all-to-all-start = ((bf16[16,144,128]{2,1,0:T(8,128)(2,1)}), bf16[16,144,128]{2,1,0:T(8,128)(2,1)S(1)}, u32[]{:S(2)}, u32[]{:S(2)}) async-start(bf16[16,144,128]{2,1,0:T(8,128)(2,1)} %bitcast.32), calls=%async_computation | async-start | bytes 1179648 | tf_op jit(solution)/shard_map/all_to_all | solution.py:53
  52.3 6.3 %shard_map.105 = (bf16[256,1024]{1,0:T(8,128)(2,1)S(1)}, f32[256,1024]{1,0:T(8,128)S(1)}) custom-call(s32[6]{0:T(128)S(1)} %stack.30.at_ref, bf16[256,2304]{1,0:T(8,128)(2,1)S(1)} %collective-permute-done.after_ref.a_ref.b_ref.g_ref, bf16[256,2304]{1,0:T(8,128)(2,1)S(1)} %collective-permute-done.after_ref.a_ref.b_ref.g_ref, bf16[256,4608]{1,0:T(8,128)(2,1)} %bitcast.34, ...), custom_call_target="tpu_custom_call" | custom-call | flops 2415919104 | bytes 7077888 | tf_op jit(solution)/shard_map/pallas_call | solution.py:80
  59.5 10.3 %collective-permute-done.6.refs_0_ = bf16[256,1024]{1,0:T(8,128)(2,1)S(1)} collective-permute-done((bf16[256,1024]{1,0:T(8,128)(2,1)}, bf16[256,1024]{1,0:T(8,128)(2,1)S(1)}, u32[]{:S(2)}, u32[]{:S(2)}) %collective-permute-start.6) | collective-permute-done | bytes 524320 | tf_op jit(solution)/shard_map/ppermute | solution.py:57
  70.6 1.7 %shard_map.107 = (bf16[16,144,128]{2,1,0:T(8,128)(2,1)}, f32[2,144,128]{2,1,0:T(8,128)}) custom-call(bf16[16,144,128]{2,1,0:T(8,128)(2,1)S(1)} %all-to-all-done.p_ref, f32[2,144,128]{2,1,0:T(8,128)S(1)} %copy.20.s_ref, bf16[256,1024]{1,0:T(8,128)(2,1)S(1)} %shard_map.106.rest_0_.gu_ref), custom_call_target="tpu_custom_call" | custom-call | flops 589824 | bytes 1179648 | tf_op jit(solution)/shard_map/pallas_call | solution.py:198
  72.4 9.3 %all-to-all-start.2 = ((bf16[16,144,128]{2,1,0:T(8,128)(2,1)}), bf16[16,144,128]{2,1,0:T(8,128)(2,1)S(1)}, u32[]{:S(2)}, u32[]{:S(2)}) async-start(bf16[16,144,128]{2,1,0:T(8,128)(2,1)} %get-tuple-element.24.after_ref), calls=%async_computation.2 | async-start | bytes 1179648 | tf_op jit(solution)/shard_map/all_to_all | solution.py:53
  84.1 14.6 %all-to-all-done.2.a_ref = bf16[16,144,128]{2,1,0:T(8,128)(2,1)S(1)} async-done(((bf16[16,144,128]{2,1,0:T(8,128)(2,1)}), bf16[16,144,128]{2,1,0:T(8,128)(2,1)S(1)}, u32[]{:S(2)}, u32[]{:S(2)}) %all-to-all-start.2) | async-done | bytes 589856 | tf_op jit(solution)/shard_map/all_to_all | solution.py:53
  98.7 1.2 collective-permute-start.11
  100.0 3.5 %collective-permute-start.12 = (bf16[16,144,128]{2,1,0:T(8,128)(2,1)S(1)}, bf16[16,144,128]{2,1,0:T(8,128)(2,1)}, u32[]{:S(2)}, u32[]{:S(2)}) collective-permute-start(bf16[16,144,128]{2,1,0:T(8,128)(2,1)S(1)} %all-to-all-done.2.a_ref), channel_id=1, source_target_pairs={{0,128},{1,129},{2,130},{3,131},{4,132},{5,133},{6,134},{7,135},{8... | collective-permute-start | bytes 1769480 | tf_op jit(solution)/shard_map/ppermute | solution.py:57
  104.4 1.2 copy-done.3
  105.6 1.9 %shard_map.108 = (bf16[256,1024]{1,0:T(8,128)(2,1)}, f32[2,144,128]{2,1,0:T(8,128)}) custom-call(f32[256,1024]{1,0:T(8,128)S(1)} %copy-done.3, bf16[256,1024]{1,0:T(8,128)(2,1)} %collective-permute-done.5.f_ref, f32[2,144,128]{2,1,0:T(8,128)} %get-tuple-element.21.outer_ref), custom_call_target="tpu_custom_call", output_to_operand_aliasing={{1}: (2, {})} | custom-call | flops 262144 | bytes 2097152 | tf_op jit(solution)/shard_map/pallas_call | solution.py:260
  107.6 1.6 %copy.21 = f32[2,144,128]{2,0,1:T(2,128)} copy(f32[2,144,128]{2,1,0:T(8,128)} %get-tuple-element.25) | data formatting | bytes 294912 | tf_op jit(solution)/shard_map/pallas_call | solution.py:260
  109.2 6.5 %all-to-all-start.3 = ((f32[8,2,18,128]{3,1,2,0:T(2,128)}), f32[8,2,18,128]{3,1,2,0:T(2,128)}, u32[]{:S(2)}, u32[]{:S(2)}) async-start(f32[8,2,18,128]{3,1,2,0:T(2,128)} %bitcast.45), calls=%async_computation.3 | async-start | bytes 294912 | tf_op jit(solution)/shard_map/all_to_all | solution.py:53
  115.7 10.6 %shard_map.109.k_ref = f32[1152,1024]{1,0:T(8,128)} custom-call(s32[6]{0:T(128)S(1)} %stack.30.at_ref, bf16[256,4608]{1,0:T(8,128)(2,1)} %bitcast.36, bf16[256,1152]{1,0:T(8,128)(2,1)S(1)} %collective-permute-done.7.n_ref, bf16[256,2304]{1,0:T(8,128)(2,1)S(1)} %collective-permute-done.after_ref.a_ref.b_ref.g_ref, ...), custom_call_target="tpu_custom_call" | custom-call | flops 2415919104 | bytes 11796480 | tf_op jit(solution)/shard_map/pallas_call | solution.py:312
  126.2 1.1 fusion
  128.7 4.8 %shard_map.110 = bf16[1152,1024]{1,0:T(8,128)(2,1)} custom-call(s32[6]{0:T(128)S(1)} %stack.30.at_ref, f32[1152,1024]{1,0:T(8,128)} %shard_map.109.k_ref, bf16[16,144,128]{2,1,0:T(8,128)(2,1)S(1)} %all-to-all-done.2.a_ref, bf16[16,144,128]{2,1,0:T(8,128)(2,1)} %collective-permute-done.11.b_ref, bf16[16,144,128]{2,1,0:T(8,128)(2,1)} %collective-permute-done.12.c_ref, ...), custom_call_target="tpu_custom_call" | custom-call | flops 2359296 | bytes 9437184 | tf_op jit(solution)/shard_map/pallas_call | solution.py:348
  (44 shorter events, 10.4 us)
Async XLA Ops:
  0.6 50.6 %collective-permute-start.1 = (bf16[1152,1024]{1,0:T(8,128)(2,1)}, bf16[1152,1024]{1,0:T(8,128)(2,1)}, u32[]{:S(2)}, u32[]{:S(2)}) collective-permute-start(bf16[1152,1024]{1,0:T(8,128)(2,1)} %bitcast.37), channel_id=1, source_target_pairs={{0,1},{1,0},{2,3},{3,2},{4,5},{5,4},{6,7},{7,6},{8,9},{9,8},{10,11... | collective-permute-start | bytes 7077896 | tf_op jit(solution)/shard_map/ppermute | solution.py:57
  0.9 13.3 %copy-start.5 = (f32[1,18,1024]{2,0,1:T(1,128)S(1)}, f32[1,18,1024]{2,0,1:T(1,128)}, u32[]{:S(2)}) copy-start(f32[1,18,1024]{2,0,1:T(1,128)} %param.13) | copy-start | bytes 221188
  0.9 13.3 %copy-start.6 = (f32[1,18,1024]{2,0,1:T(1,128)S(1)}, f32[1,18,1024]{2,0,1:T(1,128)}, u32[]{:S(2)}) copy-start(f32[1,18,1024]{2,0,1:T(1,128)} %param.12) | copy-start | bytes 221188
  6.9 32.1 %collective-permute-start = (bf16[256,2304]{1,0:T(8,128)(2,1)}, bf16[256,2304]{1,0:T(8,128)(2,1)S(1)}, u32[]{:S(2)}, u32[]{:S(2)}) collective-permute-start(bf16[256,2304]{1,0:T(8,128)(2,1)} %get-tuple-element.16), channel_id=1, source_target_pairs={{0,2},{1,3},{2,0},{3,1},{4,6},{5,7},{6,4},{7,5},{8,10},{9,11},{10,... | collective-permute-start | bytes 3538952 | tf_op jit(solution)/shard_map/ppermute | solution.py:57
  8.5 16.8 %collective-permute-start.2 = (bf16[288,1024]{1,0:T(8,128)(2,1)}, bf16[288,1024]{1,0:T(8,128)(2,1)S(1)}, u32[]{:S(2)}, u32[]{:S(2)}) collective-permute-start(bf16[288,1024]{1,0:T(8,128)(2,1)} %get-tuple-element.15.rest_0_), channel_id=1, source_target_pairs={{0,64},{1,65},{2,66},{3,67},{4,68},{5,69},{6,70},{7,71},{8,72},{9,... | collective-permute-start | bytes 1769480 | tf_op jit(solution)/shard_map/ppermute | solution.py:57
  10.0 29.0 %collective-permute-start.3 = (bf16[288,1024]{1,0:T(8,128)(2,1)}, bf16[288,1024]{1,0:T(8,128)(2,1)S(1)}, u32[]{:S(2)}, u32[]{:S(2)}) collective-permute-start(bf16[288,1024]{1,0:T(8,128)(2,1)} %get-tuple-element.17), channel_id=1, source_target_pairs={{0,128},{1,129},{2,130},{3,131},{4,132},{5,133},{6,134},{7,135},{8... | collective-permute-start | bytes 1769480 | tf_op jit(solution)/shard_map/ppermute | solution.py:57
  12.7 26.2 %collective-permute-start.4 = (bf16[288,1024]{1,0:T(8,128)(2,1)}, bf16[288,1024]{1,0:T(8,128)(2,1)S(1)}, u32[]{:S(2)}, u32[]{:S(2)}) collective-permute-start(bf16[288,1024]{1,0:T(8,128)(2,1)} %get-tuple-element.18), channel_id=1, source_target_pairs={{0,192},{1,193},{2,194},{3,195},{4,196},{5,197},{6,198},{7,199},{8... | collective-permute-start | bytes 1769480 | tf_op jit(solution)/shard_map/ppermute | solution.py:57
  15.0 25.2 %all-to-all-start.1 = ((f32[8,2,18,128]{3,1,2,0:T(2,128)}), f32[8,2,18,128]{3,1,2,0:T(2,128)S(1)}, u32[]{:S(2)}, u32[]{:S(2)}) async-start(f32[8,2,18,128]{3,1,2,0:T(2,128)} %bitcast_bitcast_fusion), calls=%async_computation.1 | async-start | bytes 294912 | tf_op jit(solution)/shard_map/all_to_all | solution.py:53
  40.1 30.5 %all-to-all-start = ((bf16[16,144,128]{2,1,0:T(8,128)(2,1)}), bf16[16,144,128]{2,1,0:T(8,128)(2,1)S(1)}, u32[]{:S(2)}, u32[]{:S(2)}) async-start(bf16[16,144,128]{2,1,0:T(8,128)(2,1)} %bitcast.32), calls=%async_computation | async-start | bytes 1179648 | tf_op jit(solution)/shard_map/all_to_all | solution.py:53
  51.1 18.8 %collective-permute-start.6 = (bf16[256,1024]{1,0:T(8,128)(2,1)}, bf16[256,1024]{1,0:T(8,128)(2,1)S(1)}, u32[]{:S(2)}, u32[]{:S(2)}) collective-permute-start(bf16[256,1024]{1,0:T(8,128)(2,1)} %bitcast.13.hu_ref), channel_id=1, source_target_pairs={{0,2},{1,3},{2,0},{3,1},{4,6},{5,7},{6,4},{7,5},{8,10},{9,11},{10,... | collective-permute-start | bytes 1572872 | tf_op jit(solution)/shard_map/ppermute | solution.py:57
  51.2 1.1 copy-start
  58.6 1.0 copy-start.2
  72.3 43.3 %copy-start.1 = (bf16[16,144,128]{2,1,0:T(8,128)(2,1)S(1)}, bf16[16,144,128]{2,1,0:T(8,128)(2,1)}, u32[]{:S(2)}) copy-start(bf16[16,144,128]{2,1,0:T(8,128)(2,1)} %get-tuple-element.24.after_ref) | copy-start | bytes 1769476
  72.4 26.4 %all-to-all-start.2 = ((bf16[16,144,128]{2,1,0:T(8,128)(2,1)}), bf16[16,144,128]{2,1,0:T(8,128)(2,1)S(1)}, u32[]{:S(2)}, u32[]{:S(2)}) async-start(bf16[16,144,128]{2,1,0:T(8,128)(2,1)} %get-tuple-element.24.after_ref), calls=%async_computation.2 | async-start | bytes 1179648 | tf_op jit(solution)/shard_map/all_to_all | solution.py:53
  81.6 2.5 %collective-permute-start.9 = (bf16[256,1024]{1,0:T(8,128)(2,1)}, bf16[256,1024]{1,0:T(8,128)(2,1)}, u32[]{:S(2)}, u32[]{:S(2)}) collective-permute-start(bf16[256,1024]{1,0:T(8,128)(2,1)} %bitcast.13.hu_ref), channel_id=1, source_target_pairs={{0,1},{1,0},{2,3},{3,2},{4,5},{5,4},{6,7},{7,6},{8,9},{9,8},{10,11... | collective-permute-start | bytes 1572872 | tf_op jit(solution)/shard_map/ppermute | solution.py:57
  81.6 18.4 %collective-permute-start.7 = (bf16[256,1152]{1,0:T(8,128)(2,1)}, bf16[256,1152]{1,0:T(8,128)(2,1)S(1)}, u32[]{:S(2)}, u32[]{:S(2)}) collective-permute-start(bf16[256,1152]{1,0:T(8,128)(2,1)} %get-tuple-element.23), channel_id=1, source_target_pairs={{0,1},{1,0},{2,3},{3,2},{4,5},{5,4},{6,7},{7,6},{8,9},{9,8},{10,11... | collective-permute-start | bytes 1769480 | tf_op jit(solution)/shard_map/ppermute | solution.py:57
  82.1 21.4 %collective-permute-start.5 = (bf16[256,1024]{1,0:T(8,128)(2,1)}, bf16[256,1024]{1,0:T(8,128)(2,1)}, u32[]{:S(2)}, u32[]{:S(2)}) collective-permute-start(bf16[256,1024]{1,0:T(8,128)(2,1)} %copy-done.4), channel_id=1, source_target_pairs={{0,2},{1,3},{2,0},{3,1},{4,6},{5,7},{6,4},{7,5},{8,10},{9,11},{10,... | collective-permute-start | bytes 1572872 | tf_op jit(solution)/shard_map/ppermute | solution.py:57
  83.6 32.1 %collective-permute-start.8 = (bf16[256,1152]{1,0:T(8,128)(2,1)}, bf16[256,1152]{1,0:T(8,128)(2,1)}, u32[]{:S(2)}, u32[]{:S(2)}) collective-permute-start(bf16[256,1152]{1,0:T(8,128)(2,1)} %constant_dynamic-slice_fusion), channel_id=1, source_target_pairs={{0,1},{1,0},{2,3},{3,2},{4,5},{5,4},{6,7},{7,6},{8,9},{9,8},{10,11... | collective-permute-start | bytes 1769480 | tf_op jit(solution)/shard_map/ppermute | solution.py:57
  83.6 32.1 %collective-permute-start.10 = (bf16[256,1024]{1,0:T(8,128)(2,1)S(1)}, bf16[256,1024]{1,0:T(8,128)(2,1)}, u32[]{:S(2)}, u32[]{:S(2)}) collective-permute-start(bf16[256,1024]{1,0:T(8,128)(2,1)S(1)} %shard_map.106.rest_0_.gu_ref), channel_id=1, source_target_pairs={{0,1},{1,0},{2,3},{3,2},{4,5},{5,4},{6,7},{7,6},{8,9},{9,8},{10,11... | collective-permute-start | bytes 1572872 | tf_op jit(solution)/shard_map/ppermute | solution.py:57
  98.7 29.9 %collective-permute-start.11 = (bf16[16,144,128]{2,1,0:T(8,128)(2,1)S(1)}, bf16[16,144,128]{2,1,0:T(8,128)(2,1)}, u32[]{:S(2)}, u32[]{:S(2)}) collective-permute-start(bf16[16,144,128]{2,1,0:T(8,128)(2,1)S(1)} %all-to-all-done.2.a_ref), channel_id=1, source_target_pairs={{0,64},{1,65},{2,66},{3,67},{4,68},{5,69},{6,70},{7,71},{8,72},{9,... | collective-permute-start | bytes 1769480 | tf_op jit(solution)/shard_map/ppermute | solution.py:57
  100.0 28.7 %collective-permute-start.12 = (bf16[16,144,128]{2,1,0:T(8,128)(2,1)S(1)}, bf16[16,144,128]{2,1,0:T(8,128)(2,1)}, u32[]{:S(2)}, u32[]{:S(2)}) collective-permute-start(bf16[16,144,128]{2,1,0:T(8,128)(2,1)S(1)} %all-to-all-done.2.a_ref), channel_id=1, source_target_pairs={{0,128},{1,129},{2,130},{3,131},{4,132},{5,133},{6,134},{7,135},{8... | collective-permute-start | bytes 1769480 | tf_op jit(solution)/shard_map/ppermute | solution.py:57
  103.5 25.1 %collective-permute-start.13 = (bf16[16,144,128]{2,1,0:T(8,128)(2,1)S(1)}, bf16[16,144,128]{2,1,0:T(8,128)(2,1)}, u32[]{:S(2)}, u32[]{:S(2)}) collective-permute-start(bf16[16,144,128]{2,1,0:T(8,128)(2,1)S(1)} %all-to-all-done.2.a_ref), channel_id=1, source_target_pairs={{0,192},{1,193},{2,194},{3,195},{4,196},{5,197},{6,198},{7,199},{8... | collective-permute-start | bytes 1769480 | tf_op jit(solution)/shard_map/ppermute | solution.py:57
  104.4 1.2 copy-start.3
  109.2 17.0 %all-to-all-start.3 = ((f32[8,2,18,128]{3,1,2,0:T(2,128)}), f32[8,2,18,128]{3,1,2,0:T(2,128)}, u32[]{:S(2)}, u32[]{:S(2)}) async-start(f32[8,2,18,128]{3,1,2,0:T(2,128)} %bitcast.45), calls=%async_computation.3 | async-start | bytes 294912 | tf_op jit(solution)/shard_map/all_to_all | solution.py:53
  (1 other events, 0.8 us)

commit v3 on v2

v3 whole, which is shorter than its diff:
```python
import jax
import jax.numpy as jnp
from jax import lax
from jax.experimental import pallas as pl
from jax.experimental.pallas import tpu as pltpu
from jax.sharding import PartitionSpec as P

beta_one = 0.9
beta_two = 0.95
bias_one = 1.0 - 0.9**8
bias_two = 1.0 - 0.95**8
inner_rate = 0.25
decay_rate = 0.1
epsilon = 1e-08
outer_rate = 0.7
outer_mu = 0.9
mixing = 0.5

NX, NYH, NZ = 4, 2, 8
NYL, NC = 2, 2
BOTH = ("rep", "fsdp")
PLANE = NYH * NZ
HZ_GROUPS = [[x * PLANE + k for k in range(PLANE)] for x in range(NX)]
BACK_GROUPS = [group[::-1] for group in HZ_GROUPS]


def pairs(move):
    found = []
    for x in range(NX):
        for h in range(NYH):
            for z in range(NZ):
                for y in range(NYL):
                    for c in range(NC):
                        x2, y2, c2 = move(x, y, c)
                        found.append(
                            (
                                ((x * NYH + h) * NZ + z) * 4 + y * 2 + c,
                                ((x2 * NYH + h) * NZ + z) * 4 + y2 * 2 + c2,
                            )
                        )
    return found


TO_OTHER_CORE = pairs(lambda x, y, c: (x, y, 1 - c))
TO_OTHER_CHIP = pairs(lambda x, y, c: (x, 1 - y, c))
TO_X = [pairs(lambda x, y, c, d=d: ((x + d) % NX, y, c)) for d in range(NX)]

MIB = 1024 * 1024
BF16, F32 = jnp.bfloat16, jnp.float32


def over(array, groups):
    return lax.all_to_all(array, "rep", 0, 0, axis_index_groups=groups)


def swap(array, to):
    return lax.ppermute(array, BOTH, to)


def dot(a, b):
    return jnp.dot(a, b, preferred_element_type=F32)


def dot_t(a, b):
    return lax.dot_general(a, b, (((0,), (0,)), ((), ())), preferred_element_type=F32)


def inside(array):
    return pltpu.with_memory_space_constraint(array, pltpu.VMEM)


def outside(array):
    return pltpu.with_memory_space_constraint(array, pltpu.HBM)


def call(kernel, grid, in_specs, out_specs, out_shape, flops, moved, at, *operands):
    spec = pltpu.PrefetchScalarGridSpec(
        num_scalar_prefetch=1, grid=grid, in_specs=in_specs, out_specs=out_specs
    )
    return pl.pallas_call(
        kernel,
        grid_spec=spec,
        out_shape=out_shape,
        compiler_params=pltpu.CompilerParams(vmem_limit_bytes=48 * MIB),
        cost_estimate=pl.CostEstimate(flops=flops, bytes_accessed=moved, transcendentals=0),
    )(at, *operands)


def cut(at, w, h):
    rows, cols = w.shape
    toks = h.shape[0]
    block, chip = rows // NX, rows * NC
    shapes = [(block, cols)] * (NX - 1) + [(toks, chip), (toks, rows)]
    count = len(shapes)

    def kernel(at_ref, w_ref, h_ref, *rest):
        outs, held, (in_sems, out_sems) = rest[:count], rest[count : 2 * count], rest[2 * count :]
        sources = []
        for d in range(1, NX):
            base = pl.multiple_of(lax.rem(at_ref[0] + d, NX) * block, 16)
            sources.append(w_ref.at[pl.ds(base, block)])
        far, near = (1 - at_ref[5]) * chip, at_ref[3] * rows
        sources.append(h_ref.at[:, pl.ds(pl.multiple_of(far, 128), chip)])
        sources.append(h_ref.at[:, pl.ds(pl.multiple_of(near, 128), rows)])
        ins = [pltpu.make_async_copy(sources[k], held[k], in_sems.at[k]) for k in range(count)]
        backs = [pltpu.make_async_copy(held[k], outs[k], out_sems.at[k]) for k in range(count)]
        for copy in ins:
            copy.start()
        for copy, back in zip(ins, backs, strict=True):
            copy.wait()
            back.start()
        for back in backs:
            back.wait()

    hbm = pl.BlockSpec(memory_space=pl.ANY)
    return pl.pallas_call(
        kernel,
        in_specs=[pl.BlockSpec(memory_space=pltpu.SMEM), hbm, hbm],
        out_specs=[hbm] * count,
        out_shape=[pltpu.HBM(x, BF16) for x in shapes],
        scratch_shapes=[pltpu.VMEM(x, BF16) for x in shapes]
        + [pltpu.SemaphoreType.DMA((count,)), pltpu.SemaphoreType.DMA((count,))],
        compiler_params=pltpu.CompilerParams(vmem_limit_bytes=12 * MIB),
    )(at, outside(w), outside(h))


def to_piece(rows_in, lane):
    return jnp.concatenate(
        [rows_in[:, c : c + lane] for c in range(0, rows_in.shape[1], lane)], axis=0
    )


def from_piece(piece, own):
    return jnp.concatenate(
        [piece[k : k + own] for k in range(0, piece.shape[0], own)], axis=1
    )


def sum_over_x(blocks, own, after):
    block, cols = blocks[0].shape
    half, lane = block // NYH, 128
    tall = own * cols // lane

    def kernel(w_ref, a_ref, b_ref, c_ref, after_ref, o_ref, held, sems):
        copies = []
        for i in range(NYH):
            rows = pl.ds(i * half, half)
            total = w_ref[rows].astype(F32) + a_ref[rows].astype(F32)
            total = total + (b_ref[rows].astype(F32) + c_ref[rows].astype(F32))
            for z in range(NZ):
                held[PLANE - 1 - i * NZ - z] = to_piece(total[z * own : (z + 1) * own], lane).astype(BF16)
            here = pl.ds((NYH - 1 - i) * NZ, NZ)
            copies.append(pltpu.make_async_copy(held.at[here], o_ref.at[here], sems.at[i]))
            copies[-1].start()
        for copy in copies:
            copy.wait()

    shape = (PLANE, tall, lane)
    return pl.pallas_call(
        kernel,
        in_specs=[pl.BlockSpec(memory_space=pltpu.VMEM)] * NX + [pl.BlockSpec(memory_space=pl.ANY)],
        out_specs=pl.BlockSpec(memory_space=pl.ANY),
        out_shape=pltpu.HBM(shape, BF16),
        scratch_shapes=[pltpu.VMEM(shape, BF16), pltpu.SemaphoreType.DMA((NYH,))],
        compiler_params=pltpu.CompilerParams(vmem_limit_bytes=16 * MIB),
    )(*[inside(x) for x in blocks], after)


def outer_step(parts, params, momenta, replicas, after):
    plane, tall, lane = parts.shape
    own = params.shape[0]

    def kernel(p_ref, g_hbm, m_hbm, after_ref, r_ref, new_ref, mom_ref, g_ref, m_ref, held, in_sems, sems):
        state = [
            pltpu.make_async_copy(g_hbm, g_ref, in_sems.at[0]),
            pltpu.make_async_copy(m_hbm, m_ref, in_sems.at[1]),
        ]
        for copy in state:
            copy.start()
        summed = p_ref[0].astype(F32)
        for k in range(1, plane):
            summed = summed + p_ref[k].astype(F32)
        summed = from_piece(summed, own)
        for copy in state:
            copy.wait()
        pseudo = g_ref[...] - summed / replicas
        momentum = outer_mu * m_ref[...] + pseudo
        renewed = g_ref[...] - outer_rate * (pseudo + outer_mu * momentum)
        held[...] = to_piece(renewed, lane).astype(BF16)
        copies = [pltpu.make_async_copy(held, r_ref.at[k], sems.at[k]) for k in range(plane)]
        for copy in copies:
            copy.start()
        new_ref[...] = renewed
        mom_ref[...] = momentum
        for copy in copies:
            copy.wait()

    vmem = pl.BlockSpec(memory_space=pltpu.VMEM)
    hbm = pl.BlockSpec(memory_space=pl.ANY)
    return pl.pallas_call(
        kernel,
        in_specs=[vmem, hbm, hbm, vmem],
        out_specs=[hbm, vmem, vmem],
        out_shape=[pltpu.HBM(parts.shape, BF16)] + [pltpu.HBM(params.shape, F32)] * 2,
        scratch_shapes=[
            pltpu.VMEM(params.shape, F32),
            pltpu.VMEM(params.shape, F32),
            pltpu.VMEM((tall, lane), BF16),
            pltpu.SemaphoreType.DMA((2,)),
            pltpu.SemaphoreType.DMA((plane,)),
        ],
        compiler_params=pltpu.CompilerParams(vmem_limit_bytes=8 * MIB),
    )(inside(parts), outside(params), outside(momenta), after)


def pack(pieces, own, after):
    plane, tall, lane = pieces.shape
    half, cols = NZ * own, tall // own * lane

    def kernel(p_ref, after_ref, o_ref, held, sems):
        copies = []
        for i in range(NYH):
            parts = [from_piece(p_ref[i * NZ + z].astype(F32), own) for z in range(NZ)]
            rows = pl.ds(i * half, half)
            held[rows] = jnp.concatenate(parts, axis=0).astype(BF16)
            copies.append(pltpu.make_async_copy(held.at[rows], o_ref.at[rows], sems.at[i]))
            copies[-1].start()
        for copy in copies:
            copy.wait()

    return pl.pallas_call(
        kernel,
        in_specs=[pl.BlockSpec(memory_space=pltpu.VMEM), pl.BlockSpec(memory_space=pl.ANY)],
        out_specs=pl.BlockSpec(memory_space=pl.ANY),
        out_shape=pltpu.HBM((NYH * half, cols), BF16),
        scratch_shapes=[pltpu.VMEM((NYH * half, cols), BF16), pltpu.SemaphoreType.DMA((NYH,))],
        compiler_params=pltpu.CompilerParams(vmem_limit_bytes=8 * MIB),
    )(inside(pieces), after)


def project(at, got, hidden, w, w_other, factor, after):
    rows, cols = w.shape
    toks = got.shape[0]
    steps = 4
    wide = cols // steps

    def kernel(at_ref, a_ref, b_ref, c_ref, d_ref, w_ref, v_ref, after_ref, far_ref, near_ref):
        far_ref[...] = ((dot(a_ref[...], w_ref[...]) + dot(b_ref[...], v_ref[...])) * factor).astype(BF16)
        near_ref[...] = (dot(c_ref[...], w_ref[...]) + dot(d_ref[...], v_ref[...])) * factor

    def left(k):
        return pl.BlockSpec((toks, rows), lambda i, at: (0, at[k]))

    column = pl.BlockSpec((toks, wide), lambda i, at: (0, i))
    wspec = pl.BlockSpec((rows, wide), lambda i, at: (0, i))
    return call(
        kernel,
        (steps,),
        [left(2), left(4), left(1), left(3), wspec, wspec, pl.BlockSpec(memory_space=pl.ANY)],
        [column, column],
        [jax.ShapeDtypeStruct((toks, cols), BF16), jax.ShapeDtypeStruct((toks, cols), F32)],
        8 * toks * rows * cols,
        4 * rows * cols + 8 * toks * rows,
        at,
        got,
        got,
        outside(hidden),
        outside(hidden),
        outside(w),
        outside(w_other),
        after,
    )


def hold(array, *after):
    hbm = pl.BlockSpec(memory_space=pl.ANY)
    small = (8, 128)

    def kernel(*refs):
        refs[-1][...] = jnp.zeros(small, F32)

    return pl.pallas_call(
        kernel,
        in_specs=[hbm] * (1 + len(after)),
        out_specs=[hbm, pl.BlockSpec(memory_space=pltpu.VMEM)],
        out_shape=[
            jax.ShapeDtypeStruct(array.shape, array.dtype),
            jax.ShapeDtypeStruct(small, F32),
        ],
        input_output_aliases={0: 0},
        compiler_params=pltpu.CompilerParams(vmem_limit_bytes=MIB),
    )(array, *after)


def finish(near, far):
    def kernel(n_ref, f_ref, o_ref):
        o_ref[...] = (n_ref[...] + f_ref[...].astype(F32)).astype(BF16)

    vmem = pl.BlockSpec(memory_space=pltpu.VMEM)
    return pl.pallas_call(
        kernel,
        in_specs=[vmem, vmem],
        out_specs=vmem,
        out_shape=jax.ShapeDtypeStruct(near.shape, BF16),
        compiler_params=pltpu.CompilerParams(vmem_limit_bytes=16 * MIB),
    )(near, far)


def inner_step(at, hidden, near, far_got, far, upstreams, w, m1, m2, factor):
    rows, cols = w.shape
    toks = hidden.shape[0]
    tall = 384
    steps = rows // tall

    def kernel(at_ref, h_ref, n_ref, g_ref, f_ref, hu_ref, nu_ref, gu_ref, fu_ref, w_ref, m1_ref, m2_ref, o_ref):
        gradient = dot_t(h_ref[...], hu_ref[...]) + dot_t(n_ref[...], nu_ref[...])
        gradient = gradient + dot_t(g_ref[...], gu_ref[...]) + dot_t(f_ref[...], fu_ref[...])
        gradient = gradient * factor
        moment_new = beta_one * m1_ref[...].astype(F32) + (1.0 - beta_one) * gradient
        second_new = beta_two * m2_ref[...].astype(F32) + (1.0 - beta_two) * gradient * gradient
        scale = jnp.sqrt(second_new * (1.0 / bias_two)) + epsilon
        stepped = moment_new * (mixing * inner_rate / bias_one) / scale
        o_ref[...] = (mixing * (1.0 - inner_rate * decay_rate)) * w_ref[...].astype(F32) - stepped

    def left(first):
        return pl.BlockSpec((toks, tall), first)

    whole = pl.BlockSpec((toks, cols), lambda i, at: (0, 0))
    own = pl.BlockSpec((tall, cols), lambda i, at: (i, 0))
    spec = pltpu.PrefetchScalarGridSpec(
        num_scalar_prefetch=1,
        grid=(steps,),
        in_specs=[
            left(lambda i, at: (0, at[1] * steps + i)),
            left(lambda i, at: (0, i)),
            left(lambda i, at: (0, at[2] * steps + i)),
            left(lambda i, at: (0, i)),
            whole,
            whole,
            whole,
            whole,
            own,
            own,
            own,
        ],
        out_specs=own,
    )
    operands = [outside(hidden), near, far_got, far] + upstreams + [outside(w), outside(m1), outside(m2)]
    return pl.pallas_call(
        kernel,
        grid_spec=spec,
        out_shape=pltpu.HBM((rows, cols), F32),
        compiler_params=pltpu.CompilerParams(vmem_limit_bytes=40 * MIB),
        cost_estimate=pl.CostEstimate(
            flops=8 * toks * rows * cols, bytes_accessed=10 * rows * cols, transcendentals=0
        ),
    )(at, *operands)


def merge(at, kept, spread):
    rows, cols = kept.shape
    block = rows // NX

    def kernel(at_ref, k_ref, a_ref, b_ref, c_ref, d_ref, o_ref, kept_ref, held, in_sems, out_sems):
        refs = [a_ref, b_ref, c_ref, d_ref]
        places = [pl.ds(pl.multiple_of(lax.rem(at_ref[0] + NX - d, NX) * block, 16), block) for d in range(NX)]
        ins = [pltpu.make_async_copy(k_ref.at[places[d]], kept_ref.at[d], in_sems.at[d]) for d in range(NX)]
        outs = [pltpu.make_async_copy(held.at[d], o_ref.at[places[d]], out_sems.at[d]) for d in range(NX)]
        for copy in ins:
            copy.start()
        for d in range(NX):
            ins[d].wait()
            new = (1.0 - mixing) * refs[d][...].astype(F32)
            held[d] = (kept_ref[d] + new).astype(BF16)
            outs[d].start()
        for copy in outs:
            copy.wait()

    vmem, hbm = pl.BlockSpec(memory_space=pltpu.VMEM), pl.BlockSpec(memory_space=pl.ANY)
    return pl.pallas_call(
        kernel,
        in_specs=[pl.BlockSpec(memory_space=pltpu.SMEM), hbm] + [vmem] * NX,
        out_specs=hbm,
        out_shape=jax.ShapeDtypeStruct((rows, cols), BF16),
        scratch_shapes=[
            pltpu.VMEM((NX, block, cols), F32),
            pltpu.VMEM((NX, block, cols), BF16),
            pltpu.SemaphoreType.DMA((NX,)),
            pltpu.SemaphoreType.DMA((NX,)),
        ],
        compiler_params=pltpu.CompilerParams(vmem_limit_bytes=24 * MIB),
        cost_estimate=pl.CostEstimate(flops=2 * rows * cols, bytes_accessed=8 * rows * cols, transcendentals=0),
    )(at, outside(kept), *[inside(x) for x in spread])


def on_device(hidden, upstream, weights, moment_one, moment_two, global_params, outer_momentum):
    width = hidden.shape[2]
    rows = weights.shape[1]
    factor = float(width) ** (-0.5)
    own = global_params.shape[1]
    block = rows // NX
    rep, fsdp = lax.axis_index("rep"), lax.axis_index("fsdp")
    core, pair = fsdp % NC, fsdp // NC
    x_at = rep // PLANE
    sibling = pair * NC + 1 - core
    at = jnp.stack([x_at, fsdp, core, sibling, 1 - core, pair]).astype(jnp.int32)
    w, h, u = weights[0], hidden[0], upstream[0]

    *sent, h_sent, h_near = cut(at, w, h)
    got = [swap(x, TO_X[d]) for d, x in enumerate(sent, 1)]

    w_other = swap(w, TO_OTHER_CORE)
    h_got = swap(h_sent, TO_OTHER_CHIP)
    h_near = swap(h_near, TO_OTHER_CORE)
    u_near = swap(u, TO_OTHER_CORE)
    h_far = swap(lax.dynamic_slice_in_dim(h_got, (1 - core) * rows, rows, 1), TO_OTHER_CORE)

    mine = lax.dynamic_slice_in_dim(w, x_at * block, block, 0)
    sum_x = sum_over_x([mine] + got, own, h_got)
    parts = over(sum_x, BACK_GROUPS)
    far_sent, near = project(at, h_got, h, w, w_other, factor, sum_x)
    u_got, token = hold(swap(u, TO_OTHER_CHIP), far_sent)
    u_far = swap(u_got, TO_OTHER_CORE)
    renewed, new_global, new_momentum = outer_step(
        parts, global_params[0], outer_momentum[0], lax.axis_size("rep"), token
    )
    corners = jnp.stack([x[:8, :128] for x in (u_far, h_far)])
    spread = [pack(over(renewed, HZ_GROUPS), own, corners)]
    for d in range(1, NX):
        spread.append(swap(spread[0], TO_X[d]))

    upstreams = [u, u_near, u_got, u_far]
    kept = inner_step(at, h, h_near, h_got, h_far, upstreams, w, moment_one[0], moment_two[0], factor)
    values = finish(near, swap(far_sent, TO_OTHER_CHIP))
    merged = merge(at, kept, spread)
    return (values[None], merged[None], new_global[None], new_momentum[None])


def solution(mesh):
    return jax.shard_map(
        on_device,
        mesh=mesh,
        in_specs=(
            P("rep", "fsdp", None),
            P("rep", "fsdp", None),
            P("rep", "fsdp", None),
            P("rep", "fsdp", None),
            P("rep", "fsdp", None),
            P("fsdp", "rep", None),
            P("fsdp", "rep", None),
        ),
        out_specs=(
            P("rep", "fsdp", None),
            P("rep", "fsdp", None),
            P("fsdp", "rep", None),
            P("fsdp", "rep", None),
        ),
        check_vma=False,
    )
```

time: 135 us -> 128 us (0.948)
  starting transfers between devices: 50 us -> 30.7 us
  waiting for transfers between devices: 39.3 us -> 54.5 us
  Pallas kernels: 32.4 us -> 30.7 us
    all_to_all x4 -> x2, starting transfers between devices: 35.2 us -> 16.7 us  [over(): return lax.all_to_all(array, 'rep', 0, 0, axis_index_groups=groups)]
    ppermute x14, waiting for transfers between devices: 24.6 us -> 40 us  [swap(): return lax.ppermute(array, BOTH, to)]
    unnamed x14 -> x19, local copies, waits for them, and re-layouts: 4.05 us -> 8.58 us
    slice x3 -> x0, local copies, waits for them, and re-layouts: 2.39 us -> none  [on_device(): return (values[None], merged[None], outer[0][None], outer[1][None])]
    pallas_call x1 -> x0, local copies, waits for them, and re-layouts: 1.65 us -> none  [finish(): pl.pallas_call(kernel, in_specs=[vmem, vmem, hbm], out_specs=[vmem, hbm],...]
    all_to_all x4 -> x2, waiting for transfers between devices: 14.6 us -> 14.6 us  [over(): return lax.all_to_all(array, 'rep', 0, 0, axis_index_groups=groups)]
  transfers between devices with their start and end apart: 18 -> 16, of which waited for: 4 -> 6; matrix products, arithmetic and copies ran while one was open for 5% -> 5% of each run, Pallas kernels for 19% -> 21%
where the time goes in v3:
time: 128 us
  waiting for transfers between devices  54.5 us (43%)
  starting transfers between devices  30.7 us (24%)
  Pallas kernels  30.7 us (24%)
  local copies, waits for them, and re-layouts  10.6 us (8%)
    ppermute x14, waiting for transfers between devices, swap(): return lax.ppermute(array, BOTH, to)  40 us
    all_to_all x2, starting transfers between devices, over(): return lax.all_to_all(array, 'rep', 0, 0, axis_index_groups=groups)  16.7 us
    all_to_all x2, waiting for transfers between devices, over(): return lax.all_to_all(array, 'rep', 0, 0, axis_index_groups=groups)  14.6 us
    ppermute x14, starting transfers between devices, swap(): return lax.ppermute(array, BOTH, to)  14 us
    pallas_call x1, Pallas kernels, inner_step(): pl.pallas_call(kernel, grid_spec=spec, out_shape=pltpu.HBM((rows, cols),...  10.2 us
    unnamed x19, local copies, waits for them, and re-layouts  8.58 us
    pallas_call x1, Pallas kernels, call(): pl.pallas_call(kernel, grid_spec=spec, out_shape=out_shape, compiler_para...  6.28 us
    pallas_call x1, Pallas kernels, merge(): pl.pallas_call(kernel, in_specs=[pl.BlockSpec(memory_space=pltpu.SMEM), h...  3.92 us
  transfers between devices with their start and end apart: 16, of which 6 were waited for; matrix products, arithmetic and copies ran while one was open for 5% of the time, Pallas kernels for 21%

profile of v3, /device:TPU:32, one launch (start us, length us, event | category | flops | bytes accessed | tf_op | source)
XLA Modules:
  0.0 127.5 jit_solution(15966414483842754508)
XLA Ops:
  0.9 3.7 %shard_map.102 = (bf16[288,1024]{1,0:T(8,128)(2,1)}, bf16[288,1024]{1,0:T(8,128)(2,1)}, bf16[288,1024]{1,0:T(8,128)(2,1)}, bf16[256,2304]{1,0:T(8,128)(2,1)}, bf16[256,1152]{1,0:T(8,128)(2,1)}) custom-call(s32[6]{0:T(128)S(1)} %stack.36.at_ref, bf16[1152,1024]{1,0:T(8,128)(2,1)} %bitcast.30, bf16[256,4608]{1,0:T(8,128)(2,1)} %bitcast.25), custom_call_target="tpu_custom_call" | custom-call | tf_op jit(solution)/shard_map/pallas_call | solution.py:116
  4.5 1.7 %collective-permute-start = (bf16[256,2304]{1,0:T(8,128)(2,1)}, bf16[256,2304]{1,0:T(8,128)(2,1)S(1)}, u32[]{:S(2)}, u32[]{:S(2)}) collective-permute-start(bf16[256,2304]{1,0:T(8,128)(2,1)} %get-tuple-element.16), channel_id=1, source_target_pairs={{0,2},{1,3},{2,0},{3,1},{4,6},{5,7},{6,4},{7,5},{8,10},{9,11},{10,... | collective-permute-start | bytes 3538952 | tf_op jit(solution)/shard_map/ppermute | solution.py:57
  6.2 1.5 %collective-permute-start.2 = (bf16[288,1024]{1,0:T(8,128)(2,1)}, bf16[288,1024]{1,0:T(8,128)(2,1)S(1)}, u32[]{:S(2)}, u32[]{:S(2)}) collective-permute-start(bf16[288,1024]{1,0:T(8,128)(2,1)} %get-tuple-element.17), channel_id=1, source_target_pairs={{0,64},{1,65},{2,66},{3,67},{4,68},{5,69},{6,70},{7,71},{8,72},{9,... | collective-permute-start | bytes 1769480 | tf_op jit(solution)/shard_map/ppermute | solution.py:57
  7.7 2.7 %collective-permute-start.3 = (bf16[288,1024]{1,0:T(8,128)(2,1)}, bf16[288,1024]{1,0:T(8,128)(2,1)S(1)}, u32[]{:S(2)}, u32[]{:S(2)}) collective-permute-start(bf16[288,1024]{1,0:T(8,128)(2,1)} %get-tuple-element.18), channel_id=1, source_target_pairs={{0,128},{1,129},{2,130},{3,131},{4,132},{5,133},{6,134},{7,135},{8... | collective-permute-start | bytes 1769480 | tf_op jit(solution)/shard_map/ppermute | solution.py:57
  10.4 1.4 %collective-permute-start.4 = (bf16[288,1024]{1,0:T(8,128)(2,1)}, bf16[288,1024]{1,0:T(8,128)(2,1)S(1)}, u32[]{:S(2)}, u32[]{:S(2)}) collective-permute-start(bf16[288,1024]{1,0:T(8,128)(2,1)} %get-tuple-element.19), channel_id=1, source_target_pairs={{0,192},{1,193},{2,194},{3,195},{4,196},{5,197},{6,198},{7,199},{8... | collective-permute-start | bytes 1769480 | tf_op jit(solution)/shard_map/ppermute | solution.py:57
  11.8 1.1 dynamic-slice_bitcast_fusion.w_ref
  13.0 10.1 %collective-permute-done.2.a_ref = bf16[288,1024]{1,0:T(8,128)(2,1)S(1)} collective-permute-done((bf16[288,1024]{1,0:T(8,128)(2,1)}, bf16[288,1024]{1,0:T(8,128)(2,1)S(1)}, u32[]{:S(2)}, u32[]{:S(2)}) %collective-permute-start.2) | collective-permute-done | bytes 589856 | tf_op jit(solution)/shard_map/ppermute | solution.py:57
  23.0 13.6 %collective-permute-done.3.b_ref = bf16[288,1024]{1,0:T(8,128)(2,1)S(1)} collective-permute-done((bf16[288,1024]{1,0:T(8,128)(2,1)}, bf16[288,1024]{1,0:T(8,128)(2,1)S(1)}, u32[]{:S(2)}, u32[]{:S(2)}) %collective-permute-start.3) | collective-permute-done | bytes 589856 | tf_op jit(solution)/shard_map/ppermute | solution.py:57
  37.7 11.3 %all-to-all-start = ((bf16[16,144,128]{2,1,0:T(8,128)(2,1)}), bf16[16,144,128]{2,1,0:T(8,128)(2,1)S(1)}, u32[]{:S(2)}, u32[]{:S(2)}) async-start(bf16[16,144,128]{2,1,0:T(8,128)(2,1)} %shard_map.103.after_ref), calls=%async_computation | async-start | bytes 1179648 | tf_op jit(solution)/shard_map/all_to_all | solution.py:53
  49.3 1.6 %copy_bitcast_fusion = (f32[18,1024]{1,0:T(8,128)}, f32[18,1024]{1,0:T(8,128)}) fusion(f32[1,18,1024]{2,0,1:T(1,128)S(1)} %copy-done.7, f32[1,18,1024]{2,0,1:T(1,128)} %param.12), kind=kLoop, calls=%fused_computation.1 | loop fusion | bytes 294912
  51.8 6.3 %shard_map.104 = (bf16[256,1024]{1,0:T(8,128)(2,1)S(1)}, f32[256,1024]{1,0:T(8,128)S(1)}) custom-call(s32[6]{0:T(128)S(1)} %stack.36.at_ref, bf16[256,2304]{1,0:T(8,128)(2,1)S(1)} %collective-permute-done.after_ref.a_ref.b_ref.g_ref, bf16[256,2304]{1,0:T(8,128)(2,1)S(1)} %collective-permute-done.after_ref.a_ref.b_ref.g_ref, bf16[256,4608]{1,0:T(8,128)(2,1)} %bitcast.26, ...), custom_call_target="tpu_custom_call" | custom-call | flops 2415919104 | bytes 7077888 | tf_op jit(solution)/shard_map/pallas_call | solution.py:80
  59.1 8.7 %collective-permute-done.9.refs_0_ = bf16[256,1024]{1,0:T(8,128)(2,1)S(1)} collective-permute-done((bf16[256,1024]{1,0:T(8,128)(2,1)}, bf16[256,1024]{1,0:T(8,128)(2,1)S(1)}, u32[]{:S(2)}, u32[]{:S(2)}) %collective-permute-start.9) | collective-permute-done | bytes 524320 | tf_op jit(solution)/shard_map/ppermute | solution.py:57
  68.5 2.6 %shard_map.108 = (bf16[16,144,128]{2,1,0:T(8,128)(2,1)}, f32[18,1024]{1,0:T(8,128)}, f32[18,1024]{1,0:T(8,128)}) custom-call(bf16[16,144,128]{2,1,0:T(8,128)(2,1)S(1)} %all-to-all-done.p_ref, f32[18,1024]{1,0:T(8,128)} %get-tuple-element.33.g_hbm, f32[18,1024]{1,0:T(8,128)} %get-tuple-element.32.m_hbm, f32[8,128]{1,0:T(8,128)S(1)} %get-tuple-element.24.after_ref), custom_call_target="tpu_custom_call" | custom-call | tf_op jit(solution)/shard_map/pallas_call | solution.py:200
  71.2 5.3 %all-to-all-start.1 = ((bf16[16,144,128]{2,1,0:T(8,128)(2,1)}), bf16[16,144,128]{2,1,0:T(8,128)(2,1)S(1)}, u32[]{:S(2)}, u32[]{:S(2)}) async-start(bf16[16,144,128]{2,1,0:T(8,128)(2,1)} %get-tuple-element.25), calls=%async_computation.1 | async-start | bytes 1179648 | tf_op jit(solution)/shard_map/all_to_all | solution.py:53
  79.2 14.6 %all-to-all-done.1.p_ref = bf16[16,144,128]{2,1,0:T(8,128)(2,1)S(1)} async-done(((bf16[16,144,128]{2,1,0:T(8,128)(2,1)}), bf16[16,144,128]{2,1,0:T(8,128)(2,1)S(1)}, u32[]{:S(2)}, u32[]{:S(2)}) %all-to-all-start.1) | async-done | bytes 589856 | tf_op jit(solution)/shard_map/all_to_all | solution.py:53
  94.8 1.3 collective-permute-start.11
  96.0 3.1 %collective-permute-start.12 = (bf16[288,1024]{1,0:T(8,128)(2,1)}, bf16[288,1024]{1,0:T(8,128)(2,1)S(1)}, u32[]{:S(2)}, u32[]{:S(2)}) collective-permute-start(bf16[288,1024]{1,0:T(8,128)(2,1)} %shard_map.109.a_ref), channel_id=1, source_target_pairs={{0,128},{1,129},{2,130},{3,131},{4,132},{5,133},{6,134},{7,135},{8... | collective-permute-start | bytes 1769480 | tf_op jit(solution)/shard_map/ppermute | solution.py:57
  99.7 1.6 %copy.12 = f32[1,18,1024]{2,0,1:T(1,128)} copy(f32[1,18,1024]{2,1,0:T(8,128)} %bitcast.38) | data formatting | bytes 147456
  101.3 1.6 %copy.13 = f32[1,18,1024]{2,0,1:T(1,128)} copy(f32[1,18,1024]{2,1,0:T(8,128)} %bitcast.37) | data formatting | bytes 147456
  102.9 1.2 copy-done.3
  104.1 1.9 %shard_map.105 = bf16[256,1024]{1,0:T(8,128)(2,1)} custom-call(f32[256,1024]{1,0:T(8,128)S(1)} %copy-done.3, bf16[256,1024]{1,0:T(8,128)(2,1)} %collective-permute-done.5.f_ref), custom_call_target="tpu_custom_call" | custom-call | tf_op jit(solution)/shard_map/pallas_call | solution.py:300
  106.1 10.2 %shard_map.107.k_ref = f32[1152,1024]{1,0:T(8,128)} custom-call(s32[6]{0:T(128)S(1)} %stack.36.at_ref, bf16[256,4608]{1,0:T(8,128)(2,1)} %bitcast.28, bf16[256,1152]{1,0:T(8,128)(2,1)S(1)} %collective-permute-done.6.n_ref, bf16[256,2304]{1,0:T(8,128)(2,1)S(1)} %collective-permute-done.after_ref.a_ref.b_ref.g_ref, ...), custom_call_target="tpu_custom_call" | custom-call | flops 2415919104 | bytes 11796480 | tf_op jit(solution)/shard_map/pallas_call | solution.py:349
  116.3 7.1 %collective-permute-done.12.c_ref = bf16[288,1024]{1,0:T(8,128)(2,1)S(1)} collective-permute-done((bf16[288,1024]{1,0:T(8,128)(2,1)}, bf16[288,1024]{1,0:T(8,128)(2,1)S(1)}, u32[]{:S(2)}, u32[]{:S(2)}) %collective-permute-start.12) | collective-permute-done | bytes 589856 | tf_op jit(solution)/shard_map/ppermute | solution.py:57
  123.5 3.9 %shard_map.110 = bf16[1152,1024]{1,0:T(8,128)(2,1)} custom-call(s32[6]{0:T(128)S(1)} %stack.36.at_ref, f32[1152,1024]{1,0:T(8,128)} %shard_map.107.k_ref, bf16[288,1024]{1,0:T(8,128)(2,1)S(1)} %copy-done.1, bf16[288,1024]{1,0:T(8,128)(2,1)S(1)} %collective-permute-done.11.b_ref, bf16[288,1024]{1,0:T(8,128)(2,1)S(1)} %collective-permute-done.12.c_ref, ...), custom_call_target="tpu_custom_call" | custom-call | flops 2359296 | bytes 9437184 | tf_op jit(solution)/shard_map/pallas_call | solution.py:380
  (42 shorter events, 8.4 us)
Async XLA Ops:
  0.6 51.2 %collective-permute-start.1 = (bf16[1152,1024]{1,0:T(8,128)(2,1)}, bf16[1152,1024]{1,0:T(8,128)(2,1)}, u32[]{:S(2)}, u32[]{:S(2)}) collective-permute-start(bf16[1152,1024]{1,0:T(8,128)(2,1)} %bitcast.29), channel_id=1, source_target_pairs={{0,1},{1,0},{2,3},{3,2},{4,5},{5,4},{6,7},{7,6},{8,9},{9,8},{10,11... | collective-permute-start | bytes 7077896 | tf_op jit(solution)/shard_map/ppermute | solution.py:57
  4.5 32.1 %collective-permute-start = (bf16[256,2304]{1,0:T(8,128)(2,1)}, bf16[256,2304]{1,0:T(8,128)(2,1)S(1)}, u32[]{:S(2)}, u32[]{:S(2)}) collective-permute-start(bf16[256,2304]{1,0:T(8,128)(2,1)} %get-tuple-element.16), channel_id=1, source_target_pairs={{0,2},{1,3},{2,0},{3,1},{4,6},{5,7},{6,4},{7,5},{8,10},{9,11},{10,... | collective-permute-start | bytes 3538952 | tf_op jit(solution)/shard_map/ppermute | solution.py:57
  6.2 16.8 %collective-permute-start.2 = (bf16[288,1024]{1,0:T(8,128)(2,1)}, bf16[288,1024]{1,0:T(8,128)(2,1)S(1)}, u32[]{:S(2)}, u32[]{:S(2)}) collective-permute-start(bf16[288,1024]{1,0:T(8,128)(2,1)} %get-tuple-element.17), channel_id=1, source_target_pairs={{0,64},{1,65},{2,66},{3,67},{4,68},{5,69},{6,70},{7,71},{8,72},{9,... | collective-permute-start | bytes 1769480 | tf_op jit(solution)/shard_map/ppermute | solution.py:57
  7.7 29.0 %collective-permute-start.3 = (bf16[288,1024]{1,0:T(8,128)(2,1)}, bf16[288,1024]{1,0:T(8,128)(2,1)S(1)}, u32[]{:S(2)}, u32[]{:S(2)}) collective-permute-start(bf16[288,1024]{1,0:T(8,128)(2,1)} %get-tuple-element.18), channel_id=1, source_target_pairs={{0,128},{1,129},{2,130},{3,131},{4,132},{5,133},{6,134},{7,135},{8... | collective-permute-start | bytes 1769480 | tf_op jit(solution)/shard_map/ppermute | solution.py:57
  10.4 26.2 %collective-permute-start.4 = (bf16[288,1024]{1,0:T(8,128)(2,1)}, bf16[288,1024]{1,0:T(8,128)(2,1)S(1)}, u32[]{:S(2)}, u32[]{:S(2)}) collective-permute-start(bf16[288,1024]{1,0:T(8,128)(2,1)} %get-tuple-element.19), channel_id=1, source_target_pairs={{0,192},{1,193},{2,194},{3,195},{4,196},{5,197},{6,198},{7,199},{8... | collective-permute-start | bytes 1769480 | tf_op jit(solution)/shard_map/ppermute | solution.py:57
  12.9 36.4 %copy-start.7 = (f32[1,18,1024]{2,0,1:T(1,128)S(1)}, f32[1,18,1024]{2,0,1:T(1,128)}, u32[]{:S(2)}) copy-start(f32[1,18,1024]{2,0,1:T(1,128)} %param.13) | copy-start | bytes 221188
  37.7 14.1 %copy-start = (bf16[16,144,128]{2,1,0:T(8,128)(2,1)S(1)}, bf16[16,144,128]{2,1,0:T(8,128)(2,1)}, u32[]{:S(2)}) copy-start(bf16[16,144,128]{2,1,0:T(8,128)(2,1)} %shard_map.103.after_ref) | copy-start | bytes 1769476
  37.7 30.8 %all-to-all-start = ((bf16[16,144,128]{2,1,0:T(8,128)(2,1)}), bf16[16,144,128]{2,1,0:T(8,128)(2,1)S(1)}, u32[]{:S(2)}, u32[]{:S(2)}) async-start(bf16[16,144,128]{2,1,0:T(8,128)(2,1)} %shard_map.103.after_ref), calls=%async_computation | async-start | bytes 1179648 | tf_op jit(solution)/shard_map/all_to_all | solution.py:53
  49.1 18.6 %collective-permute-start.9 = (bf16[256,1024]{1,0:T(8,128)(2,1)}, bf16[256,1024]{1,0:T(8,128)(2,1)S(1)}, u32[]{:S(2)}, u32[]{:S(2)}) collective-permute-start(bf16[256,1024]{1,0:T(8,128)(2,1)} %bitcast.10.hu_ref), channel_id=1, source_target_pairs={{0,2},{1,3},{2,0},{3,1},{4,6},{5,7},{6,4},{7,5},{8,10},{9,11},{10,... | collective-permute-start | bytes 1572872 | tf_op jit(solution)/shard_map/ppermute | solution.py:57
  51.8 26.2 %collective-permute-start.7 = (bf16[256,1152]{1,0:T(8,128)(2,1)}, bf16[256,1152]{1,0:T(8,128)(2,1)S(1)}, u32[]{:S(2)}, u32[]{:S(2)}) collective-permute-start(bf16[256,1152]{1,0:T(8,128)(2,1)} %constant_dynamic-slice_fusion), channel_id=1, source_target_pairs={{0,1},{1,0},{2,3},{3,2},{4,5},{5,4},{6,7},{7,6},{8,9},{9,8},{10,11... | collective-permute-start | bytes 1769480 | tf_op jit(solution)/shard_map/ppermute | solution.py:57
  58.1 1.0 copy-start.2
  67.7 0.8 copy-start.6
  71.2 22.6 %all-to-all-start.1 = ((bf16[16,144,128]{2,1,0:T(8,128)(2,1)}), bf16[16,144,128]{2,1,0:T(8,128)(2,1)S(1)}, u32[]{:S(2)}, u32[]{:S(2)}) async-start(bf16[16,144,128]{2,1,0:T(8,128)(2,1)} %get-tuple-element.25), calls=%async_computation.1 | async-start | bytes 1179648 | tf_op jit(solution)/shard_map/all_to_all | solution.py:53
  76.5 1.9 %collective-permute-start.10 = (bf16[256,1024]{1,0:T(8,128)(2,1)S(1)}, bf16[256,1024]{1,0:T(8,128)(2,1)S(1)}, u32[]{:S(2)}, u32[]{:S(2)}) collective-permute-start(bf16[256,1024]{1,0:T(8,128)(2,1)S(1)} %get-tuple-element.23.gu_ref), channel_id=1, source_target_pairs={{0,1},{1,0},{2,3},{3,2},{4,5},{5,4},{6,7},{7,6},{8,9},{9,8},{10,11... | collective-permute-start | bytes 1572872 | tf_op jit(solution)/shard_map/ppermute | solution.py:57
  76.5 29.5 %collective-permute-start.8 = (bf16[256,1024]{1,0:T(8,128)(2,1)}, bf16[256,1024]{1,0:T(8,128)(2,1)}, u32[]{:S(2)}, u32[]{:S(2)}) collective-permute-start(bf16[256,1024]{1,0:T(8,128)(2,1)} %bitcast.10.hu_ref), channel_id=1, source_target_pairs={{0,1},{1,0},{2,3},{3,2},{4,5},{5,4},{6,7},{7,6},{8,9},{9,8},{10,11... | collective-permute-start | bytes 1572872 | tf_op jit(solution)/shard_map/ppermute | solution.py:57
  77.0 29.0 %collective-permute-start.6 = (bf16[256,1152]{1,0:T(8,128)(2,1)}, bf16[256,1152]{1,0:T(8,128)(2,1)S(1)}, u32[]{:S(2)}, u32[]{:S(2)}) collective-permute-start(bf16[256,1152]{1,0:T(8,128)(2,1)} %get-tuple-element.22), channel_id=1, source_target_pairs={{0,1},{1,0},{2,3},{3,2},{4,5},{5,4},{6,7},{7,6},{8,9},{9,8},{10,11... | collective-permute-start | bytes 1769480 | tf_op jit(solution)/shard_map/ppermute | solution.py:57
  77.1 22.0 %collective-permute-start.5 = (bf16[256,1024]{1,0:T(8,128)(2,1)}, bf16[256,1024]{1,0:T(8,128)(2,1)}, u32[]{:S(2)}, u32[]{:S(2)}) collective-permute-start(bf16[256,1024]{1,0:T(8,128)(2,1)} %copy-done.6), channel_id=1, source_target_pairs={{0,2},{1,3},{2,0},{3,1},{4,6},{5,7},{6,4},{7,5},{8,10},{9,11},{10,... | collective-permute-start | bytes 1572872 | tf_op jit(solution)/shard_map/ppermute | solution.py:57
  78.4 0.8 copy-start.4
  93.8 12.3 %copy-start.5 = (bf16[256,1024]{1,0:T(8,128)(2,1)S(1)}, bf16[256,1024]{1,0:T(8,128)(2,1)}, u32[]{:S(2)}) copy-start(bf16[256,1024]{1,0:T(8,128)(2,1)} %copy-done.4) | copy-start | bytes 1572868
  94.8 21.5 %collective-permute-start.11 = (bf16[288,1024]{1,0:T(8,128)(2,1)}, bf16[288,1024]{1,0:T(8,128)(2,1)S(1)}, u32[]{:S(2)}, u32[]{:S(2)}) collective-permute-start(bf16[288,1024]{1,0:T(8,128)(2,1)} %shard_map.109.a_ref), channel_id=1, source_target_pairs={{0,64},{1,65},{2,66},{3,67},{4,68},{5,69},{6,70},{7,71},{8,72},{9,... | collective-permute-start | bytes 1769480 | tf_op jit(solution)/shard_map/ppermute | solution.py:57
  96.0 27.4 %collective-permute-start.12 = (bf16[288,1024]{1,0:T(8,128)(2,1)}, bf16[288,1024]{1,0:T(8,128)(2,1)S(1)}, u32[]{:S(2)}, u32[]{:S(2)}) collective-permute-start(bf16[288,1024]{1,0:T(8,128)(2,1)} %shard_map.109.a_ref), channel_id=1, source_target_pairs={{0,128},{1,129},{2,130},{3,131},{4,132},{5,133},{6,134},{7,135},{8... | collective-permute-start | bytes 1769480 | tf_op jit(solution)/shard_map/ppermute | solution.py:57
  99.2 24.3 %collective-permute-start.13 = (bf16[288,1024]{1,0:T(8,128)(2,1)}, bf16[288,1024]{1,0:T(8,128)(2,1)S(1)}, u32[]{:S(2)}, u32[]{:S(2)}) collective-permute-start(bf16[288,1024]{1,0:T(8,128)(2,1)} %shard_map.109.a_ref), channel_id=1, source_target_pairs={{0,192},{1,193},{2,194},{3,195},{4,196},{5,197},{6,198},{7,199},{8... | collective-permute-start | bytes 1769480 | tf_op jit(solution)/shard_map/ppermute | solution.py:57
  102.9 1.2 copy-start.3
  106.1 17.4 %copy-start.1 = (bf16[288,1024]{1,0:T(8,128)(2,1)S(1)}, bf16[288,1024]{1,0:T(8,128)(2,1)}, u32[]{:S(2)}) copy-start(bf16[288,1024]{1,0:T(8,128)(2,1)} %shard_map.109.a_ref) | copy-start | bytes 1769476

commit v4 on v3

--- a/solution.py
+++ b/solution.py
@@ -258,7 +258,7 @@
         (steps,),
         [left(2), left(4), left(1), left(3), wspec, wspec, pl.BlockSpec(memory_space=pl.ANY)],
         [column, column],
-        [jax.ShapeDtypeStruct((toks, cols), BF16), jax.ShapeDtypeStruct((toks, cols), F32)],
+        [pltpu.HBM((toks, cols), BF16), jax.ShapeDtypeStruct((toks, cols), F32)],
         8 * toks * rows * cols,
         4 * rows * cols + 8 * toks * rows,
         at,
@@ -320,7 +320,8 @@
         second_new = beta_two * m2_ref[...].astype(F32) + (1.0 - beta_two) * gradient * gradient
         scale = jnp.sqrt(second_new * (1.0 / bias_two)) + epsilon
         stepped = moment_new * (mixing * inner_rate / bias_one) / scale
-        o_ref[...] = (mixing * (1.0 - inner_rate * decay_rate)) * w_ref[...].astype(F32) - stepped
+        half = (mixing * (1.0 - inner_rate * decay_rate)) * w_ref[...].astype(F32) - stepped
+        o_ref[...] = half.astype(BF16)
 
     def left(first):
         return pl.BlockSpec((toks, tall), first)
@@ -349,7 +350,7 @@
     return pl.pallas_call(
         kernel,
         grid_spec=spec,
-        out_shape=pltpu.HBM((rows, cols), F32),
+        out_shape=pltpu.HBM((rows, cols), BF16),
         compiler_params=pltpu.CompilerParams(vmem_limit_bytes=40 * MIB),
         cost_estimate=pl.CostEstimate(
             flops=8 * toks * rows * cols, bytes_accessed=10 * rows * cols, transcendentals=0
@@ -371,7 +372,7 @@
         for d in range(NX):
             ins[d].wait()
             new = (1.0 - mixing) * refs[d][...].astype(F32)
-            held[d] = (kept_ref[d] + new).astype(BF16)
+            held[d] = (kept_ref[d].astype(F32) + new).astype(BF16)
             outs[d].start()
         for copy in outs:
             copy.wait()
@@ -383,7 +384,7 @@
         out_specs=hbm,
         out_shape=jax.ShapeDtypeStruct((rows, cols), BF16),
         scratch_shapes=[
-            pltpu.VMEM((NX, block, cols), F32),
+            pltpu.VMEM((NX, block, cols), BF16),
             pltpu.VMEM((NX, block, cols), BF16),
             pltpu.SemaphoreType.DMA((NX,)),
             pltpu.SemaphoreType.DMA((NX,)),

time: 128 us -> 128 us (level)
  no operation moved by 1% of the time
where the time goes in v4:
time: 128 us; the launch traced here: 127 us
  waiting for transfers between devices  54.1 us (42%)
  starting transfers between devices  30.7 us (24%)
  Pallas kernels  30.5 us (24%)
  local copies, waits for them, and re-layouts  10.9 us (9%)
    ppermute x14, waiting for transfers between devices, swap(): return lax.ppermute(array, BOTH, to)  39.5 us
    all_to_all x2, starting transfers between devices, over(): return lax.all_to_all(array, 'rep', 0, 0, axis_index_groups=groups)  16.7 us
    all_to_all x2, waiting for transfers between devices, over(): return lax.all_to_all(array, 'rep', 0, 0, axis_index_groups=groups)  14.6 us
    ppermute x14, starting transfers between devices, swap(): return lax.ppermute(array, BOTH, to)  14.1 us
    pallas_call x1, Pallas kernels, inner_step(): pl.pallas_call(kernel, grid_spec=spec, out_shape=pltpu.HBM((rows, cols),...  10 us
    unnamed x19, local copies, waits for them, and re-layouts  8.86 us
    pallas_call x1, Pallas kernels, call(): pl.pallas_call(kernel, grid_spec=spec, out_shape=out_shape, compiler_para...  6.87 us
    pallas_call x1, Pallas kernels, cut(): pl.pallas_call(kernel, in_specs=[pl.BlockSpec(memory_space=pltpu.SMEM), h...  3.66 us
  transfers between devices with their start and end apart: 16, of which 6 were waited for; matrix products, arithmetic and copies ran while one was open for 5% of the time, Pallas kernels for 21%

profile of v4, /device:TPU:32, one launch (start us, length us, event | category | flops | bytes accessed | tf_op | source)
XLA Modules:
  0.0 127.1 jit_solution(10113753614337192993)
XLA Ops:
  0.9 3.7 %shard_map.102 = (bf16[288,1024]{1,0:T(8,128)(2,1)}, bf16[288,1024]{1,0:T(8,128)(2,1)}, bf16[288,1024]{1,0:T(8,128)(2,1)}, bf16[256,2304]{1,0:T(8,128)(2,1)}, bf16[256,1152]{1,0:T(8,128)(2,1)}) custom-call(s32[6]{0:T(128)S(1)} %stack.36.at_ref, bf16[1152,1024]{1,0:T(8,128)(2,1)} %bitcast.30, bf16[256,4608]{1,0:T(8,128)(2,1)} %bitcast.25), custom_call_target="tpu_custom_call" | custom-call | tf_op jit(solution)/shard_map/pallas_call | solution.py:116
  4.5 1.7 %collective-permute-start = (bf16[256,2304]{1,0:T(8,128)(2,1)}, bf16[256,2304]{1,0:T(8,128)(2,1)S(1)}, u32[]{:S(2)}, u32[]{:S(2)}) collective-permute-start(bf16[256,2304]{1,0:T(8,128)(2,1)} %get-tuple-element.16), channel_id=1, source_target_pairs={{0,2},{1,3},{2,0},{3,1},{4,6},{5,7},{6,4},{7,5},{8,10},{9,11},{10,... | collective-permute-start | bytes 3538952 | tf_op jit(solution)/shard_map/ppermute | solution.py:57
  6.2 1.5 %collective-permute-start.2 = (bf16[288,1024]{1,0:T(8,128)(2,1)}, bf16[288,1024]{1,0:T(8,128)(2,1)S(1)}, u32[]{:S(2)}, u32[]{:S(2)}) collective-permute-start(bf16[288,1024]{1,0:T(8,128)(2,1)} %get-tuple-element.17), channel_id=1, source_target_pairs={{0,64},{1,65},{2,66},{3,67},{4,68},{5,69},{6,70},{7,71},{8,72},{9,... | collective-permute-start | bytes 1769480 | tf_op jit(solution)/shard_map/ppermute | solution.py:57
  7.7 2.7 %collective-permute-start.3 = (bf16[288,1024]{1,0:T(8,128)(2,1)}, bf16[288,1024]{1,0:T(8,128)(2,1)S(1)}, u32[]{:S(2)}, u32[]{:S(2)}) collective-permute-start(bf16[288,1024]{1,0:T(8,128)(2,1)} %get-tuple-element.18), channel_id=1, source_target_pairs={{0,128},{1,129},{2,130},{3,131},{4,132},{5,133},{6,134},{7,135},{8... | collective-permute-start | bytes 1769480 | tf_op jit(solution)/shard_map/ppermute | solution.py:57
  10.4 1.4 %collective-permute-start.4 = (bf16[288,1024]{1,0:T(8,128)(2,1)}, bf16[288,1024]{1,0:T(8,128)(2,1)S(1)}, u32[]{:S(2)}, u32[]{:S(2)}) collective-permute-start(bf16[288,1024]{1,0:T(8,128)(2,1)} %get-tuple-element.19), channel_id=1, source_target_pairs={{0,192},{1,193},{2,194},{3,195},{4,196},{5,197},{6,198},{7,199},{8... | collective-permute-start | bytes 1769480 | tf_op jit(solution)/shard_map/ppermute | solution.py:57
  11.8 1.1 dynamic-slice_bitcast_fusion.w_ref
  13.0 10.1 %collective-permute-done.2.a_ref = bf16[288,1024]{1,0:T(8,128)(2,1)S(1)} collective-permute-done((bf16[288,1024]{1,0:T(8,128)(2,1)}, bf16[288,1024]{1,0:T(8,128)(2,1)S(1)}, u32[]{:S(2)}, u32[]{:S(2)}) %collective-permute-start.2) | collective-permute-done | bytes 589856 | tf_op jit(solution)/shard_map/ppermute | solution.py:57
  23.0 13.6 %collective-permute-done.3.b_ref = bf16[288,1024]{1,0:T(8,128)(2,1)S(1)} collective-permute-done((bf16[288,1024]{1,0:T(8,128)(2,1)}, bf16[288,1024]{1,0:T(8,128)(2,1)S(1)}, u32[]{:S(2)}, u32[]{:S(2)}) %collective-permute-start.3) | collective-permute-done | bytes 589856 | tf_op jit(solution)/shard_map/ppermute | solution.py:57
  37.7 11.3 %all-to-all-start = ((bf16[16,144,128]{2,1,0:T(8,128)(2,1)}), bf16[16,144,128]{2,1,0:T(8,128)(2,1)S(1)}, u32[]{:S(2)}, u32[]{:S(2)}) async-start(bf16[16,144,128]{2,1,0:T(8,128)(2,1)} %shard_map.103.after_ref), calls=%async_computation | async-start | bytes 1179648 | tf_op jit(solution)/shard_map/all_to_all | solution.py:53
  49.3 1.6 %copy_bitcast_fusion = (f32[18,1024]{1,0:T(8,128)}, f32[18,1024]{1,0:T(8,128)}) fusion(f32[1,18,1024]{2,0,1:T(1,128)S(1)} %copy-done.7, f32[1,18,1024]{2,0,1:T(1,128)} %param.12), kind=kLoop, calls=%fused_computation.1 | loop fusion | bytes 294912
  51.8 6.9 %shard_map.104 = (bf16[256,1024]{1,0:T(8,128)(2,1)}, f32[256,1024]{1,0:T(8,128)S(1)}) custom-call(s32[6]{0:T(128)S(1)} %stack.36.at_ref, bf16[256,2304]{1,0:T(8,128)(2,1)S(1)} %collective-permute-done.after_ref.a_ref.b_ref.g_ref, bf16[256,2304]{1,0:T(8,128)(2,1)S(1)} %collective-permute-done.after_ref.a_ref.b_ref.g_ref, bf16[256,4608]{1,0:T(8,128)(2,1)} %bitcast.26, ...), custom_call_target="tpu_custom_call" | custom-call | flops 2415919104 | bytes 7077888 | tf_op jit(solution)/shard_map/pallas_call | solution.py:80
  59.7 8.1 %collective-permute-done.9.refs_0_ = bf16[256,1024]{1,0:T(8,128)(2,1)S(1)} collective-permute-done((bf16[256,1024]{1,0:T(8,128)(2,1)}, bf16[256,1024]{1,0:T(8,128)(2,1)S(1)}, u32[]{:S(2)}, u32[]{:S(2)}) %collective-permute-start.9) | collective-permute-done | bytes 524320 | tf_op jit(solution)/shard_map/ppermute | solution.py:57
  68.8 2.6 %shard_map.108 = (bf16[16,144,128]{2,1,0:T(8,128)(2,1)}, f32[18,1024]{1,0:T(8,128)}, f32[18,1024]{1,0:T(8,128)}) custom-call(bf16[16,144,128]{2,1,0:T(8,128)(2,1)S(1)} %all-to-all-done.p_ref, f32[18,1024]{1,0:T(8,128)} %get-tuple-element.33.g_hbm, f32[18,1024]{1,0:T(8,128)} %get-tuple-element.32.m_hbm, f32[8,128]{1,0:T(8,128)S(1)} %get-tuple-element.24.after_ref), custom_call_target="tpu_custom_call" | custom-call | tf_op jit(solution)/shard_map/pallas_call | solution.py:200
  71.4 5.3 %all-to-all-start.1 = ((bf16[16,144,128]{2,1,0:T(8,128)(2,1)}), bf16[16,144,128]{2,1,0:T(8,128)(2,1)S(1)}, u32[]{:S(2)}, u32[]{:S(2)}) async-start(bf16[16,144,128]{2,1,0:T(8,128)(2,1)} %get-tuple-element.25), calls=%async_computation.1 | async-start | bytes 1179648 | tf_op jit(solution)/shard_map/all_to_all | solution.py:53
  79.5 14.6 %all-to-all-done.1.p_ref = bf16[16,144,128]{2,1,0:T(8,128)(2,1)S(1)} async-done(((bf16[16,144,128]{2,1,0:T(8,128)(2,1)}), bf16[16,144,128]{2,1,0:T(8,128)(2,1)S(1)}, u32[]{:S(2)}, u32[]{:S(2)}) %all-to-all-start.1) | async-done | bytes 589856 | tf_op jit(solution)/shard_map/all_to_all | solution.py:53
  95.0 1.3 collective-permute-start.11
  96.3 3.1 %collective-permute-start.12 = (bf16[288,1024]{1,0:T(8,128)(2,1)}, bf16[288,1024]{1,0:T(8,128)(2,1)S(1)}, u32[]{:S(2)}, u32[]{:S(2)}) collective-permute-start(bf16[288,1024]{1,0:T(8,128)(2,1)} %shard_map.109.a_ref), channel_id=1, source_target_pairs={{0,128},{1,129},{2,130},{3,131},{4,132},{5,133},{6,134},{7,135},{8... | collective-permute-start | bytes 1769480 | tf_op jit(solution)/shard_map/ppermute | solution.py:57
  100.0 1.6 %copy.12 = f32[1,18,1024]{2,0,1:T(1,128)} copy(f32[1,18,1024]{2,1,0:T(8,128)} %bitcast.38) | data formatting | bytes 147456
  101.6 1.6 %copy.13 = f32[1,18,1024]{2,0,1:T(1,128)} copy(f32[1,18,1024]{2,1,0:T(8,128)} %bitcast.37) | data formatting | bytes 147456
  103.2 1.2 copy-done.3
  104.4 1.9 %shard_map.105 = bf16[256,1024]{1,0:T(8,128)(2,1)} custom-call(f32[256,1024]{1,0:T(8,128)S(1)} %copy-done.3, bf16[256,1024]{1,0:T(8,128)(2,1)} %collective-permute-done.5.f_ref), custom_call_target="tpu_custom_call" | custom-call | tf_op jit(solution)/shard_map/pallas_call | solution.py:300
  106.3 10.0 %shard_map.107.k_ref = bf16[1152,1024]{1,0:T(8,128)(2,1)} custom-call(s32[6]{0:T(128)S(1)} %stack.36.at_ref, bf16[256,4608]{1,0:T(8,128)(2,1)} %bitcast.28, bf16[256,1152]{1,0:T(8,128)(2,1)S(1)} %collective-permute-done.6.n_ref, bf16[256,2304]{1,0:T(8,128)(2,1)S(1)} %collective-permute-done.after_ref.a_ref.b_ref.g_ref, ...), custom_call_target="tpu_custom_call" | custom-call | flops 2415919104 | bytes 11796480 | tf_op jit(solution)/shard_map/pallas_call | solution.py:350
  116.4 7.3 %collective-permute-done.12.c_ref = bf16[288,1024]{1,0:T(8,128)(2,1)S(1)} collective-permute-done((bf16[288,1024]{1,0:T(8,128)(2,1)}, bf16[288,1024]{1,0:T(8,128)(2,1)S(1)}, u32[]{:S(2)}, u32[]{:S(2)}) %collective-permute-start.12) | collective-permute-done | bytes 589856 | tf_op jit(solution)/shard_map/ppermute | solution.py:57
  123.7 3.3 %shard_map.110 = bf16[1152,1024]{1,0:T(8,128)(2,1)} custom-call(s32[6]{0:T(128)S(1)} %stack.36.at_ref, bf16[1152,1024]{1,0:T(8,128)(2,1)} %shard_map.107.k_ref, bf16[288,1024]{1,0:T(8,128)(2,1)S(1)} %copy-done.1, bf16[288,1024]{1,0:T(8,128)(2,1)S(1)} %collective-permute-done.11.b_ref, bf16[288,1024]{1,0:T(8,128)(2,1)S(1)} %collective-permute-done.12.c_ref, ...), custom_call_target="tpu_custom_call" | custom-call | flops 2359296 | bytes 9437184 | tf_op jit(solution)/shard_map/pallas_call | solution.py:381
  (42 shorter events, 8.6 us)
Async XLA Ops:
  0.6 51.2 %collective-permute-start.1 = (bf16[1152,1024]{1,0:T(8,128)(2,1)}, bf16[1152,1024]{1,0:T(8,128)(2,1)}, u32[]{:S(2)}, u32[]{:S(2)}) collective-permute-start(bf16[1152,1024]{1,0:T(8,128)(2,1)} %bitcast.29), channel_id=1, source_target_pairs={{0,1},{1,0},{2,3},{3,2},{4,5},{5,4},{6,7},{7,6},{8,9},{9,8},{10,11... | collective-permute-start | bytes 7077896 | tf_op jit(solution)/shard_map/ppermute | solution.py:57
  4.5 32.1 %collective-permute-start = (bf16[256,2304]{1,0:T(8,128)(2,1)}, bf16[256,2304]{1,0:T(8,128)(2,1)S(1)}, u32[]{:S(2)}, u32[]{:S(2)}) collective-permute-start(bf16[256,2304]{1,0:T(8,128)(2,1)} %get-tuple-element.16), channel_id=1, source_target_pairs={{0,2},{1,3},{2,0},{3,1},{4,6},{5,7},{6,4},{7,5},{8,10},{9,11},{10,... | collective-permute-start | bytes 3538952 | tf_op jit(solution)/shard_map/ppermute | solution.py:57
  6.2 16.8 %collective-permute-start.2 = (bf16[288,1024]{1,0:T(8,128)(2,1)}, bf16[288,1024]{1,0:T(8,128)(2,1)S(1)}, u32[]{:S(2)}, u32[]{:S(2)}) collective-permute-start(bf16[288,1024]{1,0:T(8,128)(2,1)} %get-tuple-element.17), channel_id=1, source_target_pairs={{0,64},{1,65},{2,66},{3,67},{4,68},{5,69},{6,70},{7,71},{8,72},{9,... | collective-permute-start | bytes 1769480 | tf_op jit(solution)/shard_map/ppermute | solution.py:57
  7.7 29.0 %collective-permute-start.3 = (bf16[288,1024]{1,0:T(8,128)(2,1)}, bf16[288,1024]{1,0:T(8,128)(2,1)S(1)}, u32[]{:S(2)}, u32[]{:S(2)}) collective-permute-start(bf16[288,1024]{1,0:T(8,128)(2,1)} %get-tuple-element.18), channel_id=1, source_target_pairs={{0,128},{1,129},{2,130},{3,131},{4,132},{5,133},{6,134},{7,135},{8... | collective-permute-start | bytes 1769480 | tf_op jit(solution)/shard_map/ppermute | solution.py:57
  10.4 26.2 %collective-permute-start.4 = (bf16[288,1024]{1,0:T(8,128)(2,1)}, bf16[288,1024]{1,0:T(8,128)(2,1)S(1)}, u32[]{:S(2)}, u32[]{:S(2)}) collective-permute-start(bf16[288,1024]{1,0:T(8,128)(2,1)} %get-tuple-element.19), channel_id=1, source_target_pairs={{0,192},{1,193},{2,194},{3,195},{4,196},{5,197},{6,198},{7,199},{8... | collective-permute-start | bytes 1769480 | tf_op jit(solution)/shard_map/ppermute | solution.py:57
  12.9 36.4 %copy-start.7 = (f32[1,18,1024]{2,0,1:T(1,128)S(1)}, f32[1,18,1024]{2,0,1:T(1,128)}, u32[]{:S(2)}) copy-start(f32[1,18,1024]{2,0,1:T(1,128)} %param.13) | copy-start | bytes 221188
  37.7 14.1 %copy-start = (bf16[16,144,128]{2,1,0:T(8,128)(2,1)S(1)}, bf16[16,144,128]{2,1,0:T(8,128)(2,1)}, u32[]{:S(2)}) copy-start(bf16[16,144,128]{2,1,0:T(8,128)(2,1)} %shard_map.103.after_ref) | copy-start | bytes 1769476
  37.7 31.0 %all-to-all-start = ((bf16[16,144,128]{2,1,0:T(8,128)(2,1)}), bf16[16,144,128]{2,1,0:T(8,128)(2,1)S(1)}, u32[]{:S(2)}, u32[]{:S(2)}) async-start(bf16[16,144,128]{2,1,0:T(8,128)(2,1)} %shard_map.103.after_ref), calls=%async_computation | async-start | bytes 1179648 | tf_op jit(solution)/shard_map/all_to_all | solution.py:53
  49.1 18.6 %collective-permute-start.9 = (bf16[256,1024]{1,0:T(8,128)(2,1)}, bf16[256,1024]{1,0:T(8,128)(2,1)S(1)}, u32[]{:S(2)}, u32[]{:S(2)}) collective-permute-start(bf16[256,1024]{1,0:T(8,128)(2,1)} %bitcast.10.hu_ref), channel_id=1, source_target_pairs={{0,2},{1,3},{2,0},{3,1},{4,6},{5,7},{6,4},{7,5},{8,10},{9,11},{10,... | collective-permute-start | bytes 1572872 | tf_op jit(solution)/shard_map/ppermute | solution.py:57
  51.8 26.4 %collective-permute-start.7 = (bf16[256,1152]{1,0:T(8,128)(2,1)}, bf16[256,1152]{1,0:T(8,128)(2,1)S(1)}, u32[]{:S(2)}, u32[]{:S(2)}) collective-permute-start(bf16[256,1152]{1,0:T(8,128)(2,1)} %constant_dynamic-slice_fusion), channel_id=1, source_target_pairs={{0,1},{1,0},{2,3},{3,2},{4,5},{5,4},{6,7},{7,6},{8,9},{9,8},{10,11... | collective-permute-start | bytes 1769480 | tf_op jit(solution)/shard_map/ppermute | solution.py:57
  58.7 1.0 copy-start.2
  67.7 1.0 copy-start.6
  71.4 22.6 %all-to-all-start.1 = ((bf16[16,144,128]{2,1,0:T(8,128)(2,1)}), bf16[16,144,128]{2,1,0:T(8,128)(2,1)S(1)}, u32[]{:S(2)}, u32[]{:S(2)}) async-start(bf16[16,144,128]{2,1,0:T(8,128)(2,1)} %get-tuple-element.25), calls=%async_computation.1 | async-start | bytes 1179648 | tf_op jit(solution)/shard_map/all_to_all | solution.py:53
  76.8 1.9 %collective-permute-start.10 = (bf16[256,1024]{1,0:T(8,128)(2,1)S(1)}, bf16[256,1024]{1,0:T(8,128)(2,1)S(1)}, u32[]{:S(2)}, u32[]{:S(2)}) collective-permute-start(bf16[256,1024]{1,0:T(8,128)(2,1)S(1)} %get-tuple-element.23.gu_ref), channel_id=1, source_target_pairs={{0,1},{1,0},{2,3},{3,2},{4,5},{5,4},{6,7},{7,6},{8,9},{9,8},{10,11... | collective-permute-start | bytes 1572872 | tf_op jit(solution)/shard_map/ppermute | solution.py:57
  76.8 29.5 %collective-permute-start.8 = (bf16[256,1024]{1,0:T(8,128)(2,1)}, bf16[256,1024]{1,0:T(8,128)(2,1)}, u32[]{:S(2)}, u32[]{:S(2)}) collective-permute-start(bf16[256,1024]{1,0:T(8,128)(2,1)} %bitcast.10.hu_ref), channel_id=1, source_target_pairs={{0,1},{1,0},{2,3},{3,2},{4,5},{5,4},{6,7},{7,6},{8,9},{9,8},{10,11... | collective-permute-start | bytes 1572872 | tf_op jit(solution)/shard_map/ppermute | solution.py:57
  77.3 29.0 %collective-permute-start.6 = (bf16[256,1152]{1,0:T(8,128)(2,1)}, bf16[256,1152]{1,0:T(8,128)(2,1)S(1)}, u32[]{:S(2)}, u32[]{:S(2)}) collective-permute-start(bf16[256,1152]{1,0:T(8,128)(2,1)} %get-tuple-element.22), channel_id=1, source_target_pairs={{0,1},{1,0},{2,3},{3,2},{4,5},{5,4},{6,7},{7,6},{8,9},{9,8},{10,11... | collective-permute-start | bytes 1769480 | tf_op jit(solution)/shard_map/ppermute | solution.py:57
  77.4 22.0 %collective-permute-start.5 = (bf16[256,1024]{1,0:T(8,128)(2,1)}, bf16[256,1024]{1,0:T(8,128)(2,1)}, u32[]{:S(2)}, u32[]{:S(2)}) collective-permute-start(bf16[256,1024]{1,0:T(8,128)(2,1)} %get-tuple-element.21.refs_1_), channel_id=1, source_target_pairs={{0,2},{1,3},{2,0},{3,1},{4,6},{5,7},{6,4},{7,5},{8,10},{9,11},{10,... | collective-permute-start | bytes 1572872 | tf_op jit(solution)/shard_map/ppermute | solution.py:57
  78.7 0.8 copy-start.4
  94.0 12.3 %copy-start.5 = (bf16[256,1024]{1,0:T(8,128)(2,1)S(1)}, bf16[256,1024]{1,0:T(8,128)(2,1)}, u32[]{:S(2)}) copy-start(bf16[256,1024]{1,0:T(8,128)(2,1)} %copy-done.4) | copy-start | bytes 1572868
  95.0 21.4 %collective-permute-start.11 = (bf16[288,1024]{1,0:T(8,128)(2,1)}, bf16[288,1024]{1,0:T(8,128)(2,1)S(1)}, u32[]{:S(2)}, u32[]{:S(2)}) collective-permute-start(bf16[288,1024]{1,0:T(8,128)(2,1)} %shard_map.109.a_ref), channel_id=1, source_target_pairs={{0,64},{1,65},{2,66},{3,67},{4,68},{5,69},{6,70},{7,71},{8,72},{9,... | collective-permute-start | bytes 1769480 | tf_op jit(solution)/shard_map/ppermute | solution.py:57
  96.3 27.4 %collective-permute-start.12 = (bf16[288,1024]{1,0:T(8,128)(2,1)}, bf16[288,1024]{1,0:T(8,128)(2,1)S(1)}, u32[]{:S(2)}, u32[]{:S(2)}) collective-permute-start(bf16[288,1024]{1,0:T(8,128)(2,1)} %shard_map.109.a_ref), channel_id=1, source_target_pairs={{0,128},{1,129},{2,130},{3,131},{4,132},{5,133},{6,134},{7,135},{8... | collective-permute-start | bytes 1769480 | tf_op jit(solution)/shard_map/ppermute | solution.py:57
  99.4 24.3 %collective-permute-start.13 = (bf16[288,1024]{1,0:T(8,128)(2,1)}, bf16[288,1024]{1,0:T(8,128)(2,1)S(1)}, u32[]{:S(2)}, u32[]{:S(2)}) collective-permute-start(bf16[288,1024]{1,0:T(8,128)(2,1)} %shard_map.109.a_ref), channel_id=1, source_target_pairs={{0,192},{1,193},{2,194},{3,195},{4,196},{5,197},{6,198},{7,199},{8... | collective-permute-start | bytes 1769480 | tf_op jit(solution)/shard_map/ppermute | solution.py:57
  103.2 1.2 copy-start.3
  106.3 17.3 %copy-start.1 = (bf16[288,1024]{1,0:T(8,128)(2,1)S(1)}, bf16[288,1024]{1,0:T(8,128)(2,1)}, u32[]{:S(2)}) copy-start(bf16[288,1024]{1,0:T(8,128)(2,1)} %shard_map.109.a_ref) | copy-start | bytes 1769476

commit v5 on v4

--- a/solution.py
+++ b/solution.py
@@ -90,7 +90,7 @@
     rows, cols = w.shape
     toks = h.shape[0]
     block, chip = rows // NX, rows * NC
-    shapes = [(block, cols)] * (NX - 1) + [(toks, chip), (toks, rows)]
+    shapes = [(block, cols)] * (NX - 1) + [(toks, chip)]
     count = len(shapes)
 
     def kernel(at_ref, w_ref, h_ref, *rest):
@@ -99,9 +99,8 @@
         for d in range(1, NX):
             base = pl.multiple_of(lax.rem(at_ref[0] + d, NX) * block, 16)
             sources.append(w_ref.at[pl.ds(base, block)])
-        far, near = (1 - at_ref[5]) * chip, at_ref[3] * rows
+        far = (1 - at_ref[5]) * chip
         sources.append(h_ref.at[:, pl.ds(pl.multiple_of(far, 128), chip)])
-        sources.append(h_ref.at[:, pl.ds(pl.multiple_of(near, 128), rows)])
         ins = [pltpu.make_async_copy(sources[k], held[k], in_sems.at[k]) for k in range(count)]
         backs = [pltpu.make_async_copy(held[k], outs[k], out_sems.at[k]) for k in range(count)]
         for copy in ins:
@@ -407,12 +406,12 @@
     at = jnp.stack([x_at, fsdp, core, sibling, 1 - core, pair]).astype(jnp.int32)
     w, h, u = weights[0], hidden[0], upstream[0]
 
-    *sent, h_sent, h_near = cut(at, w, h)
+    *sent, h_sent = cut(at, w, h)
     got = [swap(x, TO_X[d]) for d, x in enumerate(sent, 1)]
 
     w_other = swap(w, TO_OTHER_CORE)
     h_got = swap(h_sent, TO_OTHER_CHIP)
-    h_near = swap(h_near, TO_OTHER_CORE)
+    h_near = swap(lax.dynamic_slice_in_dim(h, sibling * rows, rows, 1), TO_OTHER_CORE)
     u_near = swap(u, TO_OTHER_CORE)
     h_far = swap(lax.dynamic_slice_in_dim(h_got, (1 - core) * rows, rows, 1), TO_OTHER_CORE)
 

time: 128 us -> 128 us (level)
  waiting for transfers between devices: 54.1 us -> 50.8 us
  local copies, waits for them, and re-layouts: 10.9 us -> 12.7 us
  starting transfers between devices: 30.7 us -> 32.1 us
    ppermute x14, waiting for transfers between devices: 39.5 us -> 37.5 us  [swap(): return lax.ppermute(array, BOTH, to)]
    dynamic_slice x0 -> x1, local copies, waits for them, and re-layouts: none -> 1.94 us  [on_device(): lax.dynamic_slice_in_dim(h, sibling * rows, rows, 1)]
    ppermute x14, starting transfers between devices: 14.1 us -> 15.4 us  [swap(): return lax.ppermute(array, BOTH, to)]
    all_to_all x2, waiting for transfers between devices: 14.6 us -> 13.2 us  [over(): return lax.all_to_all(array, 'rep', 0, 0, axis_index_groups=groups)]
    unnamed x19 -> x15, local copies, waits for them, and re-layouts: 8.86 us -> 8.05 us
  transfers between devices with their start and end apart: 16 -> 16, of which waited for: 6 -> 5; matrix products, arithmetic and copies ran while one was open for 5% -> 7% of each run, Pallas kernels for 21% -> 21%
where the time goes in v5:
time: 128 us; the launch traced here: 127 us
  waiting for transfers between devices  50.8 us (40%)
  starting transfers between devices  32.1 us (25%)
  Pallas kernels  30.5 us (24%)
  local copies, waits for them, and re-layouts  12.7 us (10%)
    ppermute x14, waiting for transfers between devices, swap(): return lax.ppermute(array, BOTH, to)  37.5 us
    all_to_all x2, starting transfers between devices, over(): return lax.all_to_all(array, 'rep', 0, 0, axis_index_groups=groups)  16.7 us
    ppermute x14, starting transfers between devices, swap(): return lax.ppermute(array, BOTH, to)  15.4 us
    all_to_all x2, waiting for transfers between devices, over(): return lax.all_to_all(array, 'rep', 0, 0, axis_index_groups=groups)  13.2 us
    pallas_call x1, Pallas kernels, inner_step(): pl.pallas_call(kernel, grid_spec=spec, out_shape=pltpu.HBM((rows, cols),...  10.2 us
    unnamed x15, local copies, waits for them, and re-layouts  8.05 us
    pallas_call x1, Pallas kernels, call(): pl.pallas_call(kernel, grid_spec=spec, out_shape=out_shape, compiler_para...  6.87 us
    pallas_call x1, Pallas kernels, cut(): pl.pallas_call(kernel, in_specs=[pl.BlockSpec(memory_space=pltpu.SMEM), h...  3.44 us
  transfers between devices with their start and end apart: 16, of which 5 were waited for; matrix products, arithmetic and copies ran while one was open for 7% of the time, Pallas kernels for 21%

profile of v5, /device:TPU:32, one launch (start us, length us, event | category | flops | bytes accessed | tf_op | source)
XLA Modules:
  0.0 127.0 jit_solution(10792048342819403562)
XLA Ops:
  0.9 3.4 %shard_map.102 = (bf16[288,1024]{1,0:T(8,128)(2,1)}, bf16[288,1024]{1,0:T(8,128)(2,1)}, bf16[288,1024]{1,0:T(8,128)(2,1)}, bf16[256,2304]{1,0:T(8,128)(2,1)}) custom-call(s32[6]{0:T(128)S(1)} %stack.36.at_ref, bf16[1152,1024]{1,0:T(8,128)(2,1)} %bitcast.32, bf16[256,4608]{1,0:T(8,128)(2,1)} %bitcast.27), custom_call_target="tpu_custom_call" | custom-call | tf_op jit(solution)/shard_map/pallas_call | solution.py:115
  4.3 1.7 %collective-permute-start = (bf16[256,2304]{1,0:T(8,128)(2,1)}, bf16[256,2304]{1,0:T(8,128)(2,1)S(1)}, u32[]{:S(2)}, u32[]{:S(2)}) collective-permute-start(bf16[256,2304]{1,0:T(8,128)(2,1)} %get-tuple-element.15), channel_id=1, source_target_pairs={{0,2},{1,3},{2,0},{3,1},{4,6},{5,7},{6,4},{7,5},{8,10},{9,11},{10,... | collective-permute-start | bytes 3538952 | tf_op jit(solution)/shard_map/ppermute | solution.py:57
  6.0 1.5 %collective-permute-start.2 = (bf16[288,1024]{1,0:T(8,128)(2,1)}, bf16[288,1024]{1,0:T(8,128)(2,1)S(1)}, u32[]{:S(2)}, u32[]{:S(2)}) collective-permute-start(bf16[288,1024]{1,0:T(8,128)(2,1)} %get-tuple-element.16), channel_id=1, source_target_pairs={{0,64},{1,65},{2,66},{3,67},{4,68},{5,69},{6,70},{7,71},{8,72},{9,... | collective-permute-start | bytes 1769480 | tf_op jit(solution)/shard_map/ppermute | solution.py:57
  7.5 2.7 %collective-permute-start.3 = (bf16[288,1024]{1,0:T(8,128)(2,1)}, bf16[288,1024]{1,0:T(8,128)(2,1)S(1)}, u32[]{:S(2)}, u32[]{:S(2)}) collective-permute-start(bf16[288,1024]{1,0:T(8,128)(2,1)} %get-tuple-element.17), channel_id=1, source_target_pairs={{0,128},{1,129},{2,130},{3,131},{4,132},{5,133},{6,134},{7,135},{8... | collective-permute-start | bytes 1769480 | tf_op jit(solution)/shard_map/ppermute | solution.py:57
  10.2 1.4 %collective-permute-start.4 = (bf16[288,1024]{1,0:T(8,128)(2,1)}, bf16[288,1024]{1,0:T(8,128)(2,1)S(1)}, u32[]{:S(2)}, u32[]{:S(2)}) collective-permute-start(bf16[288,1024]{1,0:T(8,128)(2,1)} %get-tuple-element.18), channel_id=1, source_target_pairs={{0,192},{1,193},{2,194},{3,195},{4,196},{5,197},{6,198},{7,199},{8... | collective-permute-start | bytes 1769480 | tf_op jit(solution)/shard_map/ppermute | solution.py:57
  12.7 10.1 %collective-permute-done.2.a_ref = bf16[288,1024]{1,0:T(8,128)(2,1)S(1)} collective-permute-done((bf16[288,1024]{1,0:T(8,128)(2,1)}, bf16[288,1024]{1,0:T(8,128)(2,1)S(1)}, u32[]{:S(2)}, u32[]{:S(2)}) %collective-permute-start.2) | collective-permute-done | bytes 589856 | tf_op jit(solution)/shard_map/ppermute | solution.py:57
  22.8 13.6 %collective-permute-done.3.b_ref = bf16[288,1024]{1,0:T(8,128)(2,1)S(1)} collective-permute-done((bf16[288,1024]{1,0:T(8,128)(2,1)}, bf16[288,1024]{1,0:T(8,128)(2,1)S(1)}, u32[]{:S(2)}, u32[]{:S(2)}) %collective-permute-start.3) | collective-permute-done | bytes 589856 | tf_op jit(solution)/shard_map/ppermute | solution.py:57
  37.6 11.3 %all-to-all-start = ((bf16[16,144,128]{2,1,0:T(8,128)(2,1)}), bf16[16,144,128]{2,1,0:T(8,128)(2,1)S(1)}, u32[]{:S(2)}, u32[]{:S(2)}) async-start(bf16[16,144,128]{2,1,0:T(8,128)(2,1)} %shard_map.103.after_ref), calls=%async_computation | async-start | bytes 1179648 | tf_op jit(solution)/shard_map/all_to_all | solution.py:53
  49.1 1.6 %copy_bitcast_fusion = (f32[18,1024]{1,0:T(8,128)}, f32[18,1024]{1,0:T(8,128)}) fusion(f32[1,18,1024]{2,0,1:T(1,128)S(1)} %copy-done.5, f32[1,18,1024]{2,0,1:T(1,128)} %param.12), kind=kLoop, calls=%fused_computation.2 | loop fusion | bytes 294912
  51.6 6.9 %shard_map.104 = (bf16[256,1024]{1,0:T(8,128)(2,1)}, f32[256,1024]{1,0:T(8,128)S(1)}) custom-call(s32[6]{0:T(128)S(1)} %stack.36.at_ref, bf16[256,2304]{1,0:T(8,128)(2,1)S(1)} %collective-permute-done.after_ref.a_ref.b_ref.g_ref, bf16[256,2304]{1,0:T(8,128)(2,1)S(1)} %collective-permute-done.after_ref.a_ref.b_ref.g_ref, bf16[256,4608]{1,0:T(8,128)(2,1)} %bitcast.28, ...), custom_call_target="tpu_custom_call" | custom-call | flops 2415919104 | bytes 7077888 | tf_op jit(solution)/shard_map/pallas_call | solution.py:80
  59.5 8.1 %collective-permute-done.9.refs_0_ = bf16[256,1024]{1,0:T(8,128)(2,1)S(1)} collective-permute-done((bf16[256,1024]{1,0:T(8,128)(2,1)}, bf16[256,1024]{1,0:T(8,128)(2,1)S(1)}, u32[]{:S(2)}, u32[]{:S(2)}) %collective-permute-start.9) | collective-permute-done | bytes 524320 | tf_op jit(solution)/shard_map/ppermute | solution.py:57
  68.6 2.7 %shard_map.108 = (bf16[16,144,128]{2,1,0:T(8,128)(2,1)}, f32[18,1024]{1,0:T(8,128)}, f32[18,1024]{1,0:T(8,128)}) custom-call(bf16[16,144,128]{2,1,0:T(8,128)(2,1)S(1)} %all-to-all-done.p_ref, f32[18,1024]{1,0:T(8,128)} %get-tuple-element.31.g_hbm, f32[18,1024]{1,0:T(8,128)} %get-tuple-element.30.m_hbm, f32[8,128]{1,0:T(8,128)S(1)} %get-tuple-element.22.after_ref), custom_call_target="tpu_custom_call" | custom-call | tf_op jit(solution)/shard_map/pallas_call | solution.py:199
  71.3 5.3 %all-to-all-start.1 = ((bf16[16,144,128]{2,1,0:T(8,128)(2,1)}), bf16[16,144,128]{2,1,0:T(8,128)(2,1)S(1)}, u32[]{:S(2)}, u32[]{:S(2)}) async-start(bf16[16,144,128]{2,1,0:T(8,128)(2,1)} %get-tuple-element.23), calls=%async_computation.1 | async-start | bytes 1179648 | tf_op jit(solution)/shard_map/all_to_all | solution.py:53
  77.1 1.9 %dynamic-slice_bitcast_fusion = bf16[256,1152]{1,0:T(8,128)(2,1)} fusion(bf16[1,256,4608]{2,1,0:T(8,128)(2,1)} %param.7, s32[]{:T(128)S(6)} %select_n.27), kind=kLoop, calls=%fused_computation | loop fusion | bytes 1179652 | tf_op jit(solution)/shard_map/dynamic_slice | solution.py:414
  80.6 13.2 %all-to-all-done.1.p_ref = bf16[16,144,128]{2,1,0:T(8,128)(2,1)S(1)} async-done(((bf16[16,144,128]{2,1,0:T(8,128)(2,1)}), bf16[16,144,128]{2,1,0:T(8,128)(2,1)S(1)}, u32[]{:S(2)}, u32[]{:S(2)}) %all-to-all-start.1) | async-done | bytes 589856 | tf_op jit(solution)/shard_map/all_to_all | solution.py:53
  94.8 1.3 collective-permute-start.11
  96.1 3.1 %collective-permute-start.12 = (bf16[288,1024]{1,0:T(8,128)(2,1)}, bf16[288,1024]{1,0:T(8,128)(2,1)S(1)}, u32[]{:S(2)}, u32[]{:S(2)}) collective-permute-start(bf16[288,1024]{1,0:T(8,128)(2,1)} %shard_map.109.a_ref), channel_id=1, source_target_pairs={{0,128},{1,129},{2,130},{3,131},{4,132},{5,133},{6,134},{7,135},{8... | collective-permute-start | bytes 1769480 | tf_op jit(solution)/shard_map/ppermute | solution.py:57
  99.2 1.9 %collective-permute-start.13 = (bf16[288,1024]{1,0:T(8,128)(2,1)}, bf16[288,1024]{1,0:T(8,128)(2,1)S(1)}, u32[]{:S(2)}, u32[]{:S(2)}) collective-permute-start(bf16[288,1024]{1,0:T(8,128)(2,1)} %shard_map.109.a_ref), channel_id=1, source_target_pairs={{0,192},{1,193},{2,194},{3,195},{4,196},{5,197},{6,198},{7,199},{8... | collective-permute-start | bytes 1769480 | tf_op jit(solution)/shard_map/ppermute | solution.py:57
  101.2 1.6 %copy.12 = f32[1,18,1024]{2,0,1:T(1,128)} copy(f32[1,18,1024]{2,1,0:T(8,128)} %bitcast.40) | data formatting | bytes 147456
  102.8 1.6 %copy.13 = f32[1,18,1024]{2,0,1:T(1,128)} copy(f32[1,18,1024]{2,1,0:T(8,128)} %bitcast.39) | data formatting | bytes 147456
  105.6 1.9 %shard_map.105 = bf16[256,1024]{1,0:T(8,128)(2,1)} custom-call(f32[256,1024]{1,0:T(8,128)S(1)} %copy-done.3, bf16[256,1024]{1,0:T(8,128)(2,1)} %collective-permute-done.5.f_ref), custom_call_target="tpu_custom_call" | custom-call | tf_op jit(solution)/shard_map/pallas_call | solution.py:299
  107.6 10.2 %shard_map.107.k_ref = bf16[1152,1024]{1,0:T(8,128)(2,1)} custom-call(s32[6]{0:T(128)S(1)} %stack.36.at_ref, bf16[256,4608]{1,0:T(8,128)(2,1)} %bitcast.30, bf16[256,1152]{1,0:T(8,128)(2,1)S(1)} %collective-permute-done.6.n_ref, bf16[256,2304]{1,0:T(8,128)(2,1)S(1)} %collective-permute-done.after_ref.a_ref.b_ref.g_ref, ...), custom_call_target="tpu_custom_call" | custom-call | flops 2415919104 | bytes 11796480 | tf_op jit(solution)/shard_map/pallas_call | solution.py:349
  117.8 5.8 %collective-permute-done.12.c_ref = bf16[288,1024]{1,0:T(8,128)(2,1)S(1)} collective-permute-done((bf16[288,1024]{1,0:T(8,128)(2,1)}, bf16[288,1024]{1,0:T(8,128)(2,1)S(1)}, u32[]{:S(2)}, u32[]{:S(2)}) %collective-permute-start.12) | collective-permute-done | bytes 589856 | tf_op jit(solution)/shard_map/ppermute | solution.py:57
  123.5 3.3 %shard_map.110 = bf16[1152,1024]{1,0:T(8,128)(2,1)} custom-call(s32[6]{0:T(128)S(1)} %stack.36.at_ref, bf16[1152,1024]{1,0:T(8,128)(2,1)} %shard_map.107.k_ref, bf16[288,1024]{1,0:T(8,128)(2,1)S(1)} %copy-done.1, bf16[288,1024]{1,0:T(8,128)(2,1)S(1)} %collective-permute-done.11.b_ref, bf16[288,1024]{1,0:T(8,128)(2,1)S(1)} %collective-permute-done.12.c_ref, ...), custom_call_target="tpu_custom_call" | custom-call | flops 2359296 | bytes 9437184 | tf_op jit(solution)/shard_map/pallas_call | solution.py:380
  (39 shorter events, 9.8 us)
Async XLA Ops:
  0.6 51.0 %collective-permute-start.1 = (bf16[1152,1024]{1,0:T(8,128)(2,1)}, bf16[1152,1024]{1,0:T(8,128)(2,1)}, u32[]{:S(2)}, u32[]{:S(2)}) collective-permute-start(bf16[1152,1024]{1,0:T(8,128)(2,1)} %bitcast.31), channel_id=1, source_target_pairs={{0,1},{1,0},{2,3},{3,2},{4,5},{5,4},{6,7},{7,6},{8,9},{9,8},{10,11... | collective-permute-start | bytes 7077896 | tf_op jit(solution)/shard_map/ppermute | solution.py:57
  4.3 32.1 %collective-permute-start = (bf16[256,2304]{1,0:T(8,128)(2,1)}, bf16[256,2304]{1,0:T(8,128)(2,1)S(1)}, u32[]{:S(2)}, u32[]{:S(2)}) collective-permute-start(bf16[256,2304]{1,0:T(8,128)(2,1)} %get-tuple-element.15), channel_id=1, source_target_pairs={{0,2},{1,3},{2,0},{3,1},{4,6},{5,7},{6,4},{7,5},{8,10},{9,11},{10,... | collective-permute-start | bytes 3538952 | tf_op jit(solution)/shard_map/ppermute | solution.py:57
  6.0 16.8 %collective-permute-start.2 = (bf16[288,1024]{1,0:T(8,128)(2,1)}, bf16[288,1024]{1,0:T(8,128)(2,1)S(1)}, u32[]{:S(2)}, u32[]{:S(2)}) collective-permute-start(bf16[288,1024]{1,0:T(8,128)(2,1)} %get-tuple-element.16), channel_id=1, source_target_pairs={{0,64},{1,65},{2,66},{3,67},{4,68},{5,69},{6,70},{7,71},{8,72},{9,... | collective-permute-start | bytes 1769480 | tf_op jit(solution)/shard_map/ppermute | solution.py:57
  7.5 29.0 %collective-permute-start.3 = (bf16[288,1024]{1,0:T(8,128)(2,1)}, bf16[288,1024]{1,0:T(8,128)(2,1)S(1)}, u32[]{:S(2)}, u32[]{:S(2)}) collective-permute-start(bf16[288,1024]{1,0:T(8,128)(2,1)} %get-tuple-element.17), channel_id=1, source_target_pairs={{0,128},{1,129},{2,130},{3,131},{4,132},{5,133},{6,134},{7,135},{8... | collective-permute-start | bytes 1769480 | tf_op jit(solution)/shard_map/ppermute | solution.py:57
  10.2 26.2 %collective-permute-start.4 = (bf16[288,1024]{1,0:T(8,128)(2,1)}, bf16[288,1024]{1,0:T(8,128)(2,1)S(1)}, u32[]{:S(2)}, u32[]{:S(2)}) collective-permute-start(bf16[288,1024]{1,0:T(8,128)(2,1)} %get-tuple-element.18), channel_id=1, source_target_pairs={{0,192},{1,193},{2,194},{3,195},{4,196},{5,197},{6,198},{7,199},{8... | collective-permute-start | bytes 1769480 | tf_op jit(solution)/shard_map/ppermute | solution.py:57
  12.7 36.4 %copy-start.5 = (f32[1,18,1024]{2,0,1:T(1,128)S(1)}, f32[1,18,1024]{2,0,1:T(1,128)}, u32[]{:S(2)}) copy-start(f32[1,18,1024]{2,0,1:T(1,128)} %param.13) | copy-start | bytes 221188
  37.5 14.1 %copy-start = (bf16[16,144,128]{2,1,0:T(8,128)(2,1)S(1)}, bf16[16,144,128]{2,1,0:T(8,128)(2,1)}, u32[]{:S(2)}) copy-start(bf16[16,144,128]{2,1,0:T(8,128)(2,1)} %shard_map.103.after_ref) | copy-start | bytes 1769476
  37.6 31.0 %all-to-all-start = ((bf16[16,144,128]{2,1,0:T(8,128)(2,1)}), bf16[16,144,128]{2,1,0:T(8,128)(2,1)S(1)}, u32[]{:S(2)}, u32[]{:S(2)}) async-start(bf16[16,144,128]{2,1,0:T(8,128)(2,1)} %shard_map.103.after_ref), calls=%async_computation | async-start | bytes 1179648 | tf_op jit(solution)/shard_map/all_to_all | solution.py:53
  48.9 18.6 %collective-permute-start.9 = (bf16[256,1024]{1,0:T(8,128)(2,1)}, bf16[256,1024]{1,0:T(8,128)(2,1)S(1)}, u32[]{:S(2)}, u32[]{:S(2)}) collective-permute-start(bf16[256,1024]{1,0:T(8,128)(2,1)} %bitcast.11.hu_ref), channel_id=1, source_target_pairs={{0,2},{1,3},{2,0},{3,1},{4,6},{5,7},{6,4},{7,5},{8,10},{9,11},{10,... | collective-permute-start | bytes 1572872 | tf_op jit(solution)/shard_map/ppermute | solution.py:57
  51.6 28.4 %collective-permute-start.7 = (bf16[256,1152]{1,0:T(8,128)(2,1)}, bf16[256,1152]{1,0:T(8,128)(2,1)S(1)}, u32[]{:S(2)}, u32[]{:S(2)}) collective-permute-start(bf16[256,1152]{1,0:T(8,128)(2,1)} %constant_dynamic-slice_fusion), channel_id=1, source_target_pairs={{0,1},{1,0},{2,3},{3,2},{4,5},{5,4},{6,7},{7,6},{8,9},{9,8},{10,11... | collective-permute-start | bytes 1769480 | tf_op jit(solution)/shard_map/ppermute | solution.py:57
  58.5 1.0 copy-start.2
  67.5 1.0 copy-start.4
  71.3 22.6 %all-to-all-start.1 = ((bf16[16,144,128]{2,1,0:T(8,128)(2,1)}), bf16[16,144,128]{2,1,0:T(8,128)(2,1)S(1)}, u32[]{:S(2)}, u32[]{:S(2)}) async-start(bf16[16,144,128]{2,1,0:T(8,128)(2,1)} %get-tuple-element.23), calls=%async_computation.1 | async-start | bytes 1179648 | tf_op jit(solution)/shard_map/all_to_all | solution.py:53
  76.6 3.4 %collective-permute-start.10 = (bf16[256,1024]{1,0:T(8,128)(2,1)S(1)}, bf16[256,1024]{1,0:T(8,128)(2,1)}, u32[]{:S(2)}, u32[]{:S(2)}) collective-permute-start(bf16[256,1024]{1,0:T(8,128)(2,1)S(1)} %get-tuple-element.21.gu_ref), channel_id=1, source_target_pairs={{0,1},{1,0},{2,3},{3,2},{4,5},{5,4},{6,7},{7,6},{8,9},{9,8},{10,11... | collective-permute-start | bytes 1572872 | tf_op jit(solution)/shard_map/ppermute | solution.py:57
  76.6 30.9 %collective-permute-start.8 = (bf16[256,1024]{1,0:T(8,128)(2,1)}, bf16[256,1024]{1,0:T(8,128)(2,1)}, u32[]{:S(2)}, u32[]{:S(2)}) collective-permute-start(bf16[256,1024]{1,0:T(8,128)(2,1)} %bitcast.11.hu_ref), channel_id=1, source_target_pairs={{0,1},{1,0},{2,3},{3,2},{4,5},{5,4},{6,7},{7,6},{8,9},{9,8},{10,11... | collective-permute-start | bytes 1572872 | tf_op jit(solution)/shard_map/ppermute | solution.py:57
  79.1 28.5 %collective-permute-start.6 = (bf16[256,1152]{1,0:T(8,128)(2,1)}, bf16[256,1152]{1,0:T(8,128)(2,1)S(1)}, u32[]{:S(2)}, u32[]{:S(2)}) collective-permute-start(bf16[256,1152]{1,0:T(8,128)(2,1)} %dynamic-slice_bitcast_fusion), channel_id=1, source_target_pairs={{0,1},{1,0},{2,3},{3,2},{4,5},{5,4},{6,7},{7,6},{8,9},{9,8},{10,11... | collective-permute-start | bytes 1769480 | tf_op jit(solution)/shard_map/ppermute | solution.py:57
  79.2 20.1 %collective-permute-start.5 = (bf16[256,1024]{1,0:T(8,128)(2,1)}, bf16[256,1024]{1,0:T(8,128)(2,1)}, u32[]{:S(2)}, u32[]{:S(2)}) collective-permute-start(bf16[256,1024]{1,0:T(8,128)(2,1)} %get-tuple-element.20.refs_1_), channel_id=1, source_target_pairs={{0,2},{1,3},{2,0},{3,1},{4,6},{5,7},{6,4},{7,5},{8,10},{9,11},{10,... | collective-permute-start | bytes 1572872 | tf_op jit(solution)/shard_map/ppermute | solution.py:57
  94.8 22.9 %collective-permute-start.11 = (bf16[288,1024]{1,0:T(8,128)(2,1)}, bf16[288,1024]{1,0:T(8,128)(2,1)S(1)}, u32[]{:S(2)}, u32[]{:S(2)}) collective-permute-start(bf16[288,1024]{1,0:T(8,128)(2,1)} %shard_map.109.a_ref), channel_id=1, source_target_pairs={{0,64},{1,65},{2,66},{3,67},{4,68},{5,69},{6,70},{7,71},{8,72},{9,... | collective-permute-start | bytes 1769480 | tf_op jit(solution)/shard_map/ppermute | solution.py:57
  96.1 27.4 %collective-permute-start.12 = (bf16[288,1024]{1,0:T(8,128)(2,1)}, bf16[288,1024]{1,0:T(8,128)(2,1)S(1)}, u32[]{:S(2)}, u32[]{:S(2)}) collective-permute-start(bf16[288,1024]{1,0:T(8,128)(2,1)} %shard_map.109.a_ref), channel_id=1, source_target_pairs={{0,128},{1,129},{2,130},{3,131},{4,132},{5,133},{6,134},{7,135},{8... | collective-permute-start | bytes 1769480 | tf_op jit(solution)/shard_map/ppermute | solution.py:57
  99.2 24.3 %collective-permute-start.13 = (bf16[288,1024]{1,0:T(8,128)(2,1)}, bf16[288,1024]{1,0:T(8,128)(2,1)S(1)}, u32[]{:S(2)}, u32[]{:S(2)}) collective-permute-start(bf16[288,1024]{1,0:T(8,128)(2,1)} %shard_map.109.a_ref), channel_id=1, source_target_pairs={{0,192},{1,193},{2,194},{3,195},{4,196},{5,197},{6,198},{7,199},{8... | collective-permute-start | bytes 1769480 | tf_op jit(solution)/shard_map/ppermute | solution.py:57
  104.4 1.2 copy-start.3
  107.6 16.0 %copy-start.1 = (bf16[288,1024]{1,0:T(8,128)(2,1)S(1)}, bf16[288,1024]{1,0:T(8,128)(2,1)}, u32[]{:S(2)}) copy-start(bf16[288,1024]{1,0:T(8,128)(2,1)} %shard_map.109.a_ref) | copy-start | bytes 1769476
